TPU v7x, 128 devices: a whole 4x4x4 slice. The times are simulated.
128 devices in a mesh: rep: 16 (over z_hi, y, core), shard: 8 (over x, z_lo).
Axes of the slice: x: 4, y: 4, z: 4 (z_hi: 2, z_lo: 2; z = z_hi * 2 + z_lo), core: 2. Of those that a mesh axis runs over, the one named last changes fastest.
Arguments:
- tokens: bfloat16 [16384, 2048], P(('rep', 'shard')), may hold values from -6 to 6
- segments: int32 [16384], replicated, may hold values from 0 to 79, as said below
- routes: int32 [16384, 1], P(('rep', 'shard')), may hold values from 0 to 1
- gate_scores: bfloat16 [16384, 1], P(('rep', 'shard')), may hold values from 0.59765625 to 1
- attn_gain: bfloat16 [2048], P('shard'), may hold values from 0.5 to 1.5
- w_query: bfloat16 [2048, 3072], P('shard'), may hold values from -0.125 to 0.125
- w_down_kv: bfloat16 [2048, 576], P('shard'), may hold values from -0.125 to 0.125
- kv_gain: bfloat16 [512], P('shard'), may hold values from 0.5 to 1.5
- w_up_kv: bfloat16 [512, 4096], P('shard'), may hold values from -0.25 to 0.25
- w_out: bfloat16 [2048, 2048], P('shard'), may hold values from -1.5 to 1.5
- ffn_gain: bfloat16 [2048], P('shard'), may hold values from 0.5 to 1.5
- w_gate: bfloat16 [4, 2048, 1408], P(None, None, 'shard'), may hold values from -0.125 to 0.125
- w_up: bfloat16 [4, 2048, 1408], P(None, None, 'shard'), may hold values from -0.125 to 0.125
- w_down: bfloat16 [4, 1408, 2048], P(None, 'shard'), may hold values from -0.21875 to 0.21875
- cotangent: bfloat16 [16384, 2048], P(('rep', 'shard')), may hold values from -6 to 6
Outputs:
- output: bfloat16 [16384, 2048], P(('rep', 'shard'))
- tokens_grad: float32 [16384, 2048], P(('rep', 'shard'))
- attn_gain_grad: float32 [2048], P('shard')
- w_query_grad: float32 [2048, 3072], P('shard')
- w_down_kv_grad: float32 [2048, 576], P('shard')
- kv_gain_grad: float32 [512], P('shard')
- w_up_kv_grad: float32 [512, 4096], P('shard')
- w_out_grad: float32 [2048, 2048], P('shard')
- ffn_gain_grad: float32 [2048], P('shard')
- w_gate_grad: float32 [4, 2048, 1408], P(None, None, 'shard')
- w_up_grad: float32 [4, 2048, 1408], P(None, None, 'shard')
- w_down_grad: float32 [4, 1408, 2048], P(None, 'shard')
Inputs may be any that keep to these rules, and one draw needn't show every extreme that they name: `segments`: segment numbers never fall along the tokens, and no number is shared by two sequences of 1024 tokens.
All inputs are finite; a program needn't handle non-finite values.
Results may differ from a plain program's by a relative error of at most 0.025.
Values may be sent and summed in bfloat16 or wider, within the bound.
No kernel may reach another device: no remote copies, remote signals or barrier semaphores. Data moves between devices by JAX's collectives and lax.ppermute only.
A program may use at most 384 MiB of HBM per device.

v0:
```python
import jax
import jax.numpy as jnp
from jax import lax
from jax.sharding import PartitionSpec as P

H = 16
DN = 128
DR = 64
DV = 128
KVL = 512
SHARED = 2
EXPERTS = 2


norm_eps = 1e-06
rope_base = 10000.0
masked_score = -1e30


def norm_parts(values):
    inverse = lax.rsqrt(jnp.mean(values * values, axis=-1, keepdims=True) + norm_eps)
    return (values * inverse, inverse)


def norm_back(grad_normed, normed, inverse):
    return inverse * (grad_normed - normed * jnp.mean(grad_normed * normed, axis=-1, keepdims=True))


def rotary_tables(places, width):
    half_width = width // 2
    inverse = jnp.exp(
        -jnp.log(rope_base) * (2.0 * jnp.arange(half_width, dtype=jnp.float32) / width)
    )
    turns = places.astype(jnp.float32)[:, None] * inverse[None, :]
    cosine = jnp.cos(turns)
    sine_tab = jnp.sin(turns)
    return (jnp.concatenate([cosine, cosine], -1), jnp.concatenate([sine_tab, sine_tab], -1))


def turn_half(values):
    half_width = values.shape[-1] // 2
    return jnp.concatenate([-values[..., half_width:], values[..., :half_width]], -1)


def rotate(values, cosine, sine_tab):
    return values * cosine + turn_half(values) * sine_tab


def rotate_back(grads, cosine, sine_tab):
    return grads * cosine - turn_half(grads) * sine_tab


def swiglu_forward(gate_pre, up_pre, weight_cols):
    return (gate_pre * jax.nn.sigmoid(gate_pre) * up_pre * weight_cols).astype(jnp.bfloat16)


def swiglu_back(grad_hidden, gate_pre, up_pre, weight_cols):
    sigmoid_val = jax.nn.sigmoid(gate_pre)
    scaled = grad_hidden * weight_cols
    grad_gate = (scaled * up_pre * sigmoid_val * (1.0 + gate_pre * (1.0 - sigmoid_val))).astype(
        jnp.bfloat16
    )
    grad_up = (scaled * gate_pre * sigmoid_val).astype(jnp.bfloat16)
    return (grad_gate, grad_up)


def local(
    tokens,
    segments,
    routes,
    gate_scores,
    attn_gain,
    w_query,
    w_down_kv,
    kv_gain,
    w_up_kv,
    w_out,
    ffn_gain,
    w_gate,
    w_up,
    w_down,
    cotangent,
):
    row_count = tokens.shape[0]
    group_len = row_count * lax.axis_size("shard")
    shard_pos = lax.axis_index("shard")
    group_ids = lax.dynamic_slice_in_dim(segments, lax.axis_index("rep") * group_len, group_len)
    key_places = jnp.arange(group_len, dtype=jnp.int32)
    query_places = shard_pos * row_count + jnp.arange(row_count, dtype=jnp.int32)
    query_ids = lax.dynamic_slice_in_dim(group_ids, shard_pos * row_count, row_count)
    allowed = (key_places[None, :] <= query_places[:, None]) & (
        group_ids[None, :] == query_ids[:, None]
    )
    cosine, sine_tab = rotary_tables(query_places, DR)
    scale_factor = (DN + DR) ** (-0.5)

    def attention_weights():
        return (
            lax.all_gather(attn_gain, "shard", axis=0, tiled=True),
            lax.all_gather(w_query, "shard", axis=0, tiled=True),
            lax.all_gather(w_down_kv, "shard", axis=0, tiled=True),
            lax.all_gather(kv_gain, "shard", axis=0, tiled=True),
            lax.all_gather(w_up_kv, "shard", axis=0, tiled=True),
            lax.all_gather(w_out, "shard", axis=0, tiled=True),
            lax.all_gather(ffn_gain, "shard", axis=0, tiled=True),
        )

    def ffn_weights():
        return (
            lax.all_gather(w_gate, "shard", axis=2, tiled=True),
            lax.all_gather(w_up, "shard", axis=2, tiled=True),
            lax.all_gather(w_down, "shard", axis=1, tiled=True),
        )

    gain_one, query_w, down_kv_w, gain_kv, up_kv_w, out_w, gain_two = attention_weights()
    gain_one = gain_one.astype(jnp.float32)
    gain_kv = gain_kv.astype(jnp.float32)
    gain_two = gain_two.astype(jnp.float32)
    inputs_f = tokens.astype(jnp.float32)
    normed_one, inverse_one = norm_parts(inputs_f)
    normed = (normed_one * gain_one).astype(jnp.bfloat16)
    query_pre = jnp.dot(normed, query_w, preferred_element_type=jnp.float32).reshape(
        row_count, H, DN + DR
    )
    queries = jnp.concatenate(
        [
            query_pre[..., :DN],
            rotate(query_pre[..., DN:], cosine[:, None, :], sine_tab[:, None, :]),
        ],
        -1,
    ).astype(jnp.bfloat16)
    latent_all = jnp.dot(normed, down_kv_w, preferred_element_type=jnp.float32)
    latent_normed, latent_inverse = norm_parts(latent_all[:, :KVL])
    latent = (latent_normed * gain_kv).astype(jnp.bfloat16)
    key_rope = rotate(latent_all[:, KVL:], cosine, sine_tab).astype(jnp.bfloat16)
    key_value = jnp.dot(latent, up_kv_w, preferred_element_type=jnp.float32).astype(jnp.bfloat16)
    kv_group, rope_group = (
        lax.all_gather(key_value, "shard", axis=0, tiled=True),
        lax.all_gather(key_rope, "shard", axis=0, tiled=True),
    )
    kv_heads = kv_group.reshape(group_len, H, DN + DV)
    key_nope = kv_heads[..., :DN]
    values = kv_heads[..., DN:]

    def masked_scores():
        raw_scores = jnp.einsum(
            "ihd,jhd->hij", queries[..., :DN], key_nope, preferred_element_type=jnp.float32
        )
        raw_scores = raw_scores + jnp.einsum(
            "ihd,jd->hij", queries[..., DN:], rope_group, preferred_element_type=jnp.float32
        )
        return jnp.where(allowed[None], raw_scores * scale_factor, masked_score)

    scores = masked_scores()
    row_max = jnp.max(scores, axis=-1, keepdims=True)
    expo = jnp.exp(scores - row_max)
    row_total = jnp.sum(expo, axis=-1, keepdims=True)
    log_total = row_max + jnp.log(row_total)
    attention = (expo / row_total).astype(jnp.bfloat16)
    context = jnp.einsum("hij,jhd->ihd", attention, values, preferred_element_type=jnp.float32)
    context = context.reshape(row_count, H * DV).astype(jnp.bfloat16)
    residual = inputs_f + jnp.dot(context, out_w, preferred_element_type=jnp.float32)
    normed_two, inverse_two = norm_parts(residual)
    ffn_in = (normed_two * gain_two).astype(jnp.bfloat16)
    chosen = routes[:, :, None] == jnp.arange(EXPERTS, dtype=jnp.int32)[None, None, :]
    routed = jnp.sum(jnp.where(chosen, gate_scores.astype(jnp.float32)[:, :, None], 0.0), axis=1)
    combine = jnp.concatenate([jnp.ones((row_count, SHARED), jnp.float32), routed], axis=1)
    gate_all, up_all, down_all = ffn_weights()
    weight_cols = combine.T[:, :, None]
    gate_pre = jnp.einsum("td,edf->etf", ffn_in, gate_all, preferred_element_type=jnp.float32)
    up_pre = jnp.einsum("td,edf->etf", ffn_in, up_all, preferred_element_type=jnp.float32)
    hidden_units = swiglu_forward(gate_pre, up_pre, weight_cols)
    output = residual + jnp.einsum(
        "etf,efd->td", hidden_units, down_all, preferred_element_type=jnp.float32
    )
    grad_out = cotangent.astype(jnp.float32)
    gate_all, up_all, down_all = ffn_weights()
    grad_hidden = jnp.einsum("td,efd->etf", cotangent, down_all, preferred_element_type=jnp.float32)
    grad_gate, grad_up = swiglu_back(grad_hidden, gate_pre, up_pre, weight_cols)
    gate_full = jnp.einsum("td,etf->edf", ffn_in, grad_gate, preferred_element_type=jnp.float32)
    up_full = jnp.einsum("td,etf->edf", ffn_in, grad_up, preferred_element_type=jnp.float32)
    down_full = jnp.einsum(
        "etf,td->efd", hidden_units, cotangent, preferred_element_type=jnp.float32
    )
    grad_ffn_in = jnp.einsum(
        "etf,edf->td", grad_gate, gate_all, preferred_element_type=jnp.float32
    ) + jnp.einsum("etf,edf->td", grad_up, up_all, preferred_element_type=jnp.float32)
    gate_grad, up_grad, down_grad = (
        lax.psum_scatter(
            gate_full.astype(jnp.bfloat16), "shard", scatter_dimension=2, tiled=True
        ).astype(jnp.float32),
        lax.psum_scatter(
            up_full.astype(jnp.bfloat16), "shard", scatter_dimension=2, tiled=True
        ).astype(jnp.float32),
        lax.psum_scatter(
            down_full.astype(jnp.bfloat16), "shard", scatter_dimension=1, tiled=True
        ).astype(jnp.float32),
    )
    gain_two_part = jnp.sum(grad_ffn_in * normed_two, axis=0)
    grad_residual = grad_out + norm_back(grad_ffn_in * gain_two, normed_two, inverse_two)
    gain_one_b, query_w, down_kv_w, gain_kv_b, up_kv_w, out_w, gain_two_b = attention_weights()
    grad_branch = grad_residual.astype(jnp.bfloat16)
    out_part = jnp.einsum("ti,td->id", context, grad_branch, preferred_element_type=jnp.float32)
    grad_context = jnp.einsum("td,id->ti", grad_branch, out_w, preferred_element_type=jnp.float32)
    grad_context = grad_context.astype(jnp.bfloat16).reshape(row_count, H, DV)
    probs = jnp.exp(masked_scores() - log_total)
    attention_back = probs.astype(jnp.bfloat16)
    grad_probs = jnp.einsum(
        "ihd,jhd->hij", grad_context, values, preferred_element_type=jnp.float32
    )
    row_dot = jnp.sum(probs * grad_probs, axis=-1, keepdims=True)
    grad_scores = (probs * (grad_probs - row_dot)).astype(jnp.bfloat16)
    grad_query_nope = (
        jnp.einsum("hij,jhd->ihd", grad_scores, key_nope, preferred_element_type=jnp.float32)
        * scale_factor
    )
    grad_query_rope = (
        jnp.einsum("hij,jd->ihd", grad_scores, rope_group, preferred_element_type=jnp.float32)
        * scale_factor
    )
    grad_key_nope = (
        jnp.einsum(
            "hij,ihd->jhd", grad_scores, queries[..., :DN], preferred_element_type=jnp.float32
        )
        * scale_factor
    )
    grad_key_rope = (
        jnp.einsum(
            "hij,ihd->jd", grad_scores, queries[..., DN:], preferred_element_type=jnp.float32
        )
        * scale_factor
    )
    grad_values = jnp.einsum(
        "hij,ihd->jhd", attention_back, grad_context, preferred_element_type=jnp.float32
    )
    grad_kv_group = jnp.concatenate([grad_key_nope, grad_values], -1).reshape(
        group_len, H * (DN + DV)
    )
    grad_kv_own, grad_rope_own = (
        lax.psum_scatter(
            grad_kv_group.astype(jnp.bfloat16), "shard", scatter_dimension=0, tiled=True
        ).astype(jnp.float32),
        lax.psum_scatter(
            grad_key_rope.astype(jnp.bfloat16), "shard", scatter_dimension=0, tiled=True
        ).astype(jnp.float32),
    )
    grad_key_value = grad_kv_own.astype(jnp.bfloat16)
    up_kv_part = jnp.einsum("tc,tk->ck", latent, grad_key_value, preferred_element_type=jnp.float32)
    grad_latent = jnp.einsum(
        "tk,ck->tc", grad_key_value, up_kv_w, preferred_element_type=jnp.float32
    )
    gain_kv_part = jnp.sum(grad_latent * latent_normed, axis=0)
    grad_latent_pre = norm_back(grad_latent * gain_kv, latent_normed, latent_inverse)
    grad_latent_all = jnp.concatenate(
        [grad_latent_pre, rotate_back(grad_rope_own, cosine, sine_tab)], -1
    ).astype(jnp.bfloat16)
    grad_query_pre = jnp.concatenate(
        [grad_query_nope, rotate_back(grad_query_rope, cosine[:, None, :], sine_tab[:, None, :])],
        -1,
    )
    grad_query_pre = grad_query_pre.reshape(row_count, H * (DN + DR)).astype(jnp.bfloat16)
    query_part = jnp.einsum("td,tk->dk", normed, grad_query_pre, preferred_element_type=jnp.float32)
    down_kv_part = jnp.einsum(
        "td,tk->dk", normed, grad_latent_all, preferred_element_type=jnp.float32
    )
    grad_normed = jnp.einsum(
        "tk,dk->td", grad_query_pre, query_w, preferred_element_type=jnp.float32
    ) + jnp.einsum("tk,dk->td", grad_latent_all, down_kv_w, preferred_element_type=jnp.float32)
    gain_one_part = jnp.sum(grad_normed * normed_one, axis=0)
    tokens_grad = grad_residual + norm_back(grad_normed * gain_one, normed_one, inverse_one)
    gain_one_grad, query_grad, down_kv_grad, gain_kv_grad, up_kv_grad, out_grad, gain_two_grad = (
        lax.psum_scatter(
            gain_one_part.astype(jnp.bfloat16), "shard", scatter_dimension=0, tiled=True
        ).astype(jnp.float32),
        lax.psum_scatter(
            query_part.astype(jnp.bfloat16), "shard", scatter_dimension=0, tiled=True
        ).astype(jnp.float32),
        lax.psum_scatter(
            down_kv_part.astype(jnp.bfloat16), "shard", scatter_dimension=0, tiled=True
        ).astype(jnp.float32),
        lax.psum_scatter(
            gain_kv_part.astype(jnp.bfloat16), "shard", scatter_dimension=0, tiled=True
        ).astype(jnp.float32),
        lax.psum_scatter(
            up_kv_part.astype(jnp.bfloat16), "shard", scatter_dimension=0, tiled=True
        ).astype(jnp.float32),
        lax.psum_scatter(
            out_part.astype(jnp.bfloat16), "shard", scatter_dimension=0, tiled=True
        ).astype(jnp.float32),
        lax.psum_scatter(
            gain_two_part.astype(jnp.bfloat16), "shard", scatter_dimension=0, tiled=True
        ).astype(jnp.float32),
    )
    totals = (
        lax.psum(gain_one_grad.astype(jnp.bfloat16), "rep").astype(jnp.float32),
        lax.psum(query_grad.astype(jnp.bfloat16), "rep").astype(jnp.float32),
        lax.psum(down_kv_grad.astype(jnp.bfloat16), "rep").astype(jnp.float32),
        lax.psum(gain_kv_grad.astype(jnp.bfloat16), "rep").astype(jnp.float32),
        lax.psum(up_kv_grad.astype(jnp.bfloat16), "rep").astype(jnp.float32),
        lax.psum(out_grad.astype(jnp.bfloat16), "rep").astype(jnp.float32),
        lax.psum(gain_two_grad.astype(jnp.bfloat16), "rep").astype(jnp.float32),
        lax.psum(gate_grad.astype(jnp.bfloat16), "rep").astype(jnp.float32),
        lax.psum(up_grad.astype(jnp.bfloat16), "rep").astype(jnp.float32),
        lax.psum(down_grad.astype(jnp.bfloat16), "rep").astype(jnp.float32),
    )
    return (
        output.astype(jnp.bfloat16),
        tokens_grad,
        totals[0],
        totals[1],
        totals[2],
        totals[3],
        totals[4],
        totals[5],
        totals[6],
        totals[7],
        totals[8],
        totals[9],
    )


def solution(mesh):
    in_specs = (
        P(("rep", "shard"), None),
        P(),
        P(("rep", "shard"), None),
        P(("rep", "shard"), None),
        P("shard"),
        P("shard", None),
        P("shard", None),
        P("shard"),
        P("shard", None),
        P("shard", None),
        P("shard"),
        P(None, None, "shard"),
        P(None, None, "shard"),
        P(None, "shard", None),
        P(("rep", "shard"), None),
    )
    out_specs = (
        P(("rep", "shard"), None),
        P(("rep", "shard"), None),
        P("shard"),
        P("shard", None),
        P("shard", None),
        P("shard"),
        P("shard", None),
        P("shard", None),
        P("shard"),
        P(None, None, "shard"),
        P(None, None, "shard"),
        P(None, "shard", None),
    )
    return jax.shard_map(local, mesh=mesh, in_specs=in_specs, out_specs=out_specs, check_vma=False)
```

profile of v0, /device:TPU:0, one launch (start us, length us, event | category | flops | bytes accessed | tf_op | source)
XLA Modules:
  0.0 4520.6 jit_solution(4012990198114811569)
XLA Ops:
  12.2 20.4 all-reduce.1
  32.7 15.7 all-gather
  49.7 26.3 all-gather.11.cloned.1.call-done
  78.8 94.1 %all-gather.13.cloned.1.call-done = bf16[512,4096]{1,0:T(8,128)(2,1)} async-done(((bf16[64,4096]{1,0:T(8,128)(2,1)}), bf16[512,4096]{1,0:T(8,128)(2,1)}) %all-gather.13.cloned.1.call-update) | async-done | bytes 4194320 | tf_op jit(solution)/shard_map/all_gather | solution.py:103
  181.7 24.0 all-gather.1
  206.2 32.5 all_gather.49
  238.8 111.8 %all-gather.15.cloned.1.call-done = bf16[1024,4096]{1,0:T(8,128)(2,1)} async-done(((bf16[128,4096]{1,0:T(8,128)(2,1)}), bf16[1024,4096]{1,0:T(8,128)(2,1)}) %all-gather.15.cloned.1.call-update) | async-done | bytes 8388624 | tf_op jit(solution)/shard_map/all_gather | solution.py:138
  373.5 228.7 %all-gather.17.cloned.1.call-done = bf16[2048,3072]{1,0:T(8,128)(2,1)} async-done(((bf16[256,3072]{1,0:T(8,128)(2,1)}), bf16[2048,3072]{1,0:T(8,128)(2,1)}) %all-gather.17.cloned.1.call-update) | async-done | bytes 12582928 | tf_op jit(solution)/shard_map/all_gather | solution.py:100
  624.4 148.6 %all-gather.19.cloned.1.call-done = bf16[2048,2048]{1,0:T(8,128)(2,1)} async-done(((bf16[256,2048]{1,0:T(8,128)(2,1)}), bf16[2048,2048]{1,0:T(8,128)(2,1)}) %all-gather.19.cloned.1.call-update) | async-done | bytes 8388624 | tf_op jit(solution)/shard_map/all_gather | solution.py:104
  778.6 445.0 %all-gather.23.cloned.1.call-done = bf16[4,2048,1408]{1,2,0:T(8,128)(2,1)} async-done(((bf16[4,2048,176]{1,2,0:T(8,128)(2,1)}), bf16[4,2048,1408]{1,2,0:T(8,128)(2,1)}) %all-gather.23.cloned.1.call-update) | async-done | bytes 23068688 | tf_op jit(solution)/shard_map/all_gather | solution.py:111
  1237.6 432.4 %all-gather.25.cloned.1.call-done = bf16[4,1408,2048]{2,1,0:T(8,128)(2,1)} async-done(((bf16[4,176,2048]{2,1,0:T(8,128)(2,1)}), bf16[4,1408,2048]{2,1,0:T(8,128)(2,1)}) %all-gather.25.cloned.1.call-update) | async-done | bytes 23068688 | tf_op jit(solution)/shard_map/all_gather | solution.py:112
  1670.0 16.8 fusion.15
  1686.9 429.5 %all-gather.21.cloned.1.call-done = bf16[4,2048,1408]{1,2,0:T(8,128)(2,1)} async-done(((bf16[4,2048,176]{1,2,0:T(8,128)(2,1)}), bf16[4,2048,1408]{1,2,0:T(8,128)(2,1)}) %all-gather.21.cloned.1.call-update) | async-done | bytes 23068688 | tf_op jit(solution)/shard_map/all_gather | solution.py:110
  2219.2 169.3 %reduce-scatter.28.cloned.1.call-done = bf16[128,4096]{1,0:T(8,128)(2,1)} async-done(((bf16[1024,4096]{1,0:T(8,128)(2,1)}), bf16[128,4096]{1,0:T(8,128)(2,1)}) %reduce-scatter.28.cloned.1.call-update) | async-done | bytes 1048592
  2455.7 105.6 %reduce-scatter.20.cloned.1.call-done = bf16[256,2048]{1,0:T(8,128)(2,1)} async-done(((bf16[2048,2048]{1,0:T(8,128)(2,1)}), bf16[256,2048]{1,0:T(8,128)(2,1)}) %reduce-scatter.20.cloned.1.call-update) | async-done | bytes 1048592 | tf_op jit(solution)/shard_map/reduce_scatter | solution.py:287
  2561.2 60.2 %reduce-scatter.16.cloned.1.call-done = bf16[256,576]{0,1:T(8,128)(2,1)} async-done(((bf16[2048,576]{0,1:T(8,128)(2,1)}), bf16[256,576]{0,1:T(8,128)(2,1)}) %reduce-scatter.16.cloned.1.call-update) | async-done | bytes 294928 | tf_op jit(solution)/shard_map/reduce_scatter | solution.py:278
  2621.4 94.3 %reduce-scatter.18.cloned.1.call-done = bf16[64,4096]{1,0:T(8,128)(2,1)} async-done(((bf16[512,4096]{1,0:T(8,128)(2,1)}), bf16[64,4096]{1,0:T(8,128)(2,1)}) %reduce-scatter.18.cloned.1.call-update) | async-done | bytes 524304 | tf_op jit(solution)/shard_map/reduce_scatter | solution.py:284
  2715.8 251.6 %reduce-scatter.14.cloned.1.call-done = bf16[256,3072]{1,0:T(8,128)(2,1)} async-done(((bf16[2048,3072]{1,0:T(8,128)(2,1)}), bf16[256,3072]{1,0:T(8,128)(2,1)}) %reduce-scatter.14.cloned.1.call-update) | async-done | bytes 1572880 | tf_op jit(solution)/shard_map/reduce_scatter | solution.py:275
  2967.3 448.1 %reduce-scatter.26.cloned.1.call-done = bf16[4,176,2048]{2,1,0:T(8,128)(2,1)} async-done(((bf16[4,1408,2048]{2,1,0:T(8,128)(2,1)}), bf16[4,176,2048]{2,1,0:T(8,128)(2,1)}) %reduce-scatter.26.cloned.1.call-update) | async-done | bytes 2883600 | tf_op jit(solution)/shard_map/reduce_scatter | solution.py:195
  3415.5 448.1 %reduce-scatter.22.cloned.1.call-done = bf16[4,2048,176]{1,2,0:T(8,128)(2,1)} async-done(((bf16[4,2048,1408]{1,2,0:T(8,128)(2,1)}), bf16[4,2048,176]{1,2,0:T(8,128)(2,1)}) %reduce-scatter.22.cloned.1.call-update) | async-done | bytes 2883600 | tf_op jit(solution)/shard_map/reduce_scatter | solution.py:189
  3863.6 448.1 %reduce-scatter.24.cloned.1.call-done = bf16[4,2048,176]{1,2,0:T(8,128)(2,1)} async-done(((bf16[4,2048,1408]{1,2,0:T(8,128)(2,1)}), bf16[4,2048,176]{1,2,0:T(8,128)(2,1)}) %reduce-scatter.24.cloned.1.call-update) | async-done | bytes 2883600 | tf_op jit(solution)/shard_map/reduce_scatter | solution.py:192
  4336.0 21.1 all-reduce.7
  4357.3 33.4 all-reduce.5
  4394.9 99.3 %all-reduce.10.cloned.1.call-done = (bf16[256,3072]{1,0:T(8,128)(2,1)}, bf16[256,576]{0,1:T(8,128)(2,1)}, bf16[64,4096]{1,0:T(8,128)(2,1)}, bf16[256,2048]{1,0:T...) async-done(((bf16[256,3072]{1,0:T(8,128)(2,1)}, bf16[256,576]{0,1:T(8,128)(2,1)}, ...) | async-done | bytes 12091408 | tf_op jit(solution)/shard_map/psum | solution.py:296
  (239 shorter events, 297.9 us)
Async XLA Ops:
  7.2 68.8 %all-gather.11.cloned.1.call-start = ((), (), s32[]{:S(2)}) async-start(), calls=%async_computation.9 | async-start | bytes 2654208 | tf_op jit(solution)/shard_map/all_gather | solution.py:101
  7.9 165.0 %all-gather.13.cloned.1.call-start = ((), (), s32[]{:S(2)}) async-start(), calls=%async_computation.10 | async-start | bytes 4718592 | tf_op jit(solution)/shard_map/all_gather | solution.py:103
  8.7 341.9 %all-gather.15.cloned.1.call-start = ((), (), s32[]{:S(2)}) async-start(), calls=%async_computation.11 | async-start | bytes 9437184 | tf_op jit(solution)/shard_map/all_gather | solution.py:138
  49.7 552.5 %copy-start.38 = (f32[128]{0:T(128)}, f32[128]{0:T(128)S(1)}, u32[]{:S(2)}) copy-start(f32[128]{0:T(128)S(1)} %add_rsqrt_fusion.2) | copy-start | bytes 1540
  176.9 425.3 %all-gather.17.cloned.1.call-start = ((), (), s32[]{:S(2)}) async-start(), calls=%async_computation.12 | async-start | bytes 14155776 | tf_op jit(solution)/shard_map/all_gather | solution.py:100
  177.5 595.6 %all-gather.19.cloned.1.call-start = ((), (), s32[]{:S(2)}) async-start(), calls=%async_computation.13 | async-start | bytes 9437184 | tf_op jit(solution)/shard_map/all_gather | solution.py:104
  178.1 1045.6 %all-gather.23.cloned.1.call-start = ((), (), s32[]{:S(2)}) async-start(), calls=%async_computation.15 | async-start | bytes 25952256 | tf_op jit(solution)/shard_map/all_gather | solution.py:111
  178.7 1491.4 %all-gather.25.cloned.1.call-start = ((), (), s32[]{:S(2)}) async-start(), calls=%async_computation.16 | async-start | bytes 25952256 | tf_op jit(solution)/shard_map/all_gather | solution.py:112
  179.4 1937.0 %all-gather.21.cloned.1.call-start = ((), (), s32[]{:S(2)}) async-start(), calls=%async_computation.14 | async-start | bytes 25952256 | tf_op jit(solution)/shard_map/all_gather | solution.py:110
  180.2 2038.1 %reduce-scatter.30.cloned.1.call-start = ((), (), s32[]{:S(2)}) async-start(), calls=%async_computation.25 | async-start | bytes 294912
  205.8 1464.2 %copy-start.45 = (f32[4,128]{1,0:T(4,128)}, f32[4,128]{1,0:T(4,128)S(1)}, u32[]{:S(2)}) copy-start(f32[4,128]{1,0:T(4,128)S(1)} %pad_bitcast_fusion) | copy-start | bytes 6148
  206.2 404.1 %copy-start.29 = (f32[128,64]{0,1:T(8,128)}, f32[128,64]{0,1:T(8,128)S(1)}, u32[]{:S(2)}) copy-start(f32[128,64]{0,1:T(8,128)S(1)} %get-tuple-element.45) | copy-start | bytes 98308
  238.8 371.6 %copy-start.26 = (bf16[1024,64]{0,1:T(8,128)(2,1)}, bf16[1024,64]{0,1:T(8,128)(2,1)S(1)}, u32[]{:S(2)}) copy-start(bf16[1024,64]{0,1:T(8,128)(2,1)S(1)} %all_gather.49) | copy-start | bytes 393220
  366.8 235.4 %copy-start.3 = (bf16[128,2048]{1,0:T(8,128)(2,1)S(1)}, bf16[128,2048]{1,0:T(8,128)(2,1)}, u32[]{:S(2)}) copy-start(bf16[128,2048]{1,0:T(8,128)(2,1)} %param.15) | copy-start | bytes 1572868
  778.6 891.4 %copy-start.22 = (bf16[128,2048]{1,0:T(8,128)(2,1)S(1)}, bf16[128,2048]{1,0:T(8,128)(2,1)}, u32[]{:S(2)}) copy-start(bf16[128,2048]{1,0:T(8,128)(2,1)} %param.29) | copy-start | bytes 1572868
  2179.9 208.6 %reduce-scatter.28.cloned.1.call-start = ((), (), s32[]{:S(2)}) async-start(), calls=%async_computation.24 | async-start | bytes 9437184
  2200.1 361.1 %reduce-scatter.20.cloned.1.call-start = ((), (), s32[]{:S(2)}) async-start(), calls=%async_computation.20 | async-start | bytes 9437184 | tf_op jit(solution)/shard_map/reduce_scatter | solution.py:287
  2206.9 414.6 %reduce-scatter.16.cloned.1.call-start = ((), (), s32[]{:S(2)}) async-start(), calls=%async_computation.18 | async-start | bytes 2654208 | tf_op jit(solution)/shard_map/reduce_scatter | solution.py:278
  2396.2 319.6 %reduce-scatter.18.cloned.1.call-start = ((), (), s32[]{:S(2)}) async-start(), calls=%async_computation.19 | async-start | bytes 4718592 | tf_op jit(solution)/shard_map/reduce_scatter | solution.py:284
  2400.8 566.5 %reduce-scatter.14.cloned.1.call-start = ((), (), s32[]{:S(2)}) async-start(), calls=%async_computation.17 | async-start | bytes 14155776 | tf_op jit(solution)/shard_map/reduce_scatter | solution.py:275
  2418.1 997.4 %reduce-scatter.26.cloned.1.call-start = ((), (), s32[]{:S(2)}) async-start(), calls=%async_computation.23 | async-start | bytes 25952256 | tf_op jit(solution)/shard_map/reduce_scatter | solution.py:195
  2430.4 1433.2 %reduce-scatter.22.cloned.1.call-start = ((), (), s32[]{:S(2)}) async-start(), calls=%async_computation.21 | async-start | bytes 25952256 | tf_op jit(solution)/shard_map/reduce_scatter | solution.py:189
  2442.8 1868.9 %reduce-scatter.24.cloned.1.call-start = ((), (), s32[]{:S(2)}) async-start(), calls=%async_computation.22 | async-start | bytes 25952256 | tf_op jit(solution)/shard_map/reduce_scatter | solution.py:192
  2455.6 2038.6 %all-reduce.10.cloned.1.call-start = ((), (), s32[]{:S(2)}) async-start(), calls=%async_computation.26 | async-start | bytes 24182784 | tf_op jit(solution)/shard_map/psum | solution.py:296
  (47 other events, 1654.9 us)
Sparse Core Ops, SparseCore 0:
  9.6 66.3 all-gather.10
  77.6 95.1 all-gather.12
  177.0 173.4 all-gather.14
  352.0 250.0 all-gather.16
  603.7 169.3 all-gather.18
  774.6 449.0 all-gather.22
  1225.3 444.6 all-gather.24
  1671.7 444.6 all-gather.20
  2180.0 38.2 reduce-scatter.29
  2220.7 167.7 reduce-scatter.27
  2391.0 170.1 reduce-scatter.19
  2564.2 57.1 reduce-scatter.15
  2624.6 91.1 reduce-scatter.17
  2718.2 249.1 reduce-scatter.13
  2969.8 445.6 reduce-scatter.25
  3417.9 445.6 reduce-scatter.21
  3866.1 445.6 reduce-scatter.23
  4315.0 179.1 all-reduce.9
where the time goes:
time: 4530 us; the launch traced here: 4520 us
  waiting for transfers between devices  4060 us (90%)
  matrix products  208 us (5%)
  blocking collectives  147 us (3%)
  local copies, waits for them, and re-layouts  50.4 us (1%)
    reduce_scatter x1, waiting for transfers between devices, local(): lax.psum_scatter(gate_full.astype(jnp.bfloat16), 'shard', scatter_dimensi...  448 us
    reduce_scatter x1, waiting for transfers between devices, local(): lax.psum_scatter(up_full.astype(jnp.bfloat16), 'shard', scatter_dimension...  448 us
    reduce_scatter x1, waiting for transfers between devices, local(): lax.psum_scatter(down_full.astype(jnp.bfloat16), 'shard', scatter_dimensi...  448 us
    all_gather x1, waiting for transfers between devices, ffn_weights(): lax.all_gather(w_up, 'shard', axis=2, tiled=True)  445 us
    all_gather x1, waiting for transfers between devices, ffn_weights(): lax.all_gather(w_down, 'shard', axis=1, tiled=True)  432 us
    all_gather x1, waiting for transfers between devices, ffn_weights(): lax.all_gather(w_gate, 'shard', axis=2, tiled=True)  430 us
    reduce_scatter x1, waiting for transfers between devices, local(): lax.psum_scatter(query_part.astype(jnp.bfloat16), 'shard', scatter_dimens...  252 us
    all_gather x1, waiting for transfers between devices, attention_weights(): lax.all_gather(w_query, 'shard', axis=0, tiled=True)  229 us
  transfers between devices with their start and end apart: 18, of which 18 were waited for; matrix products, arithmetic and copies ran while one was open for 5% of the time, Pallas kernels for 0%

commit v1 on v0

v1 whole, which is shorter than its diff:
```python
import functools

import jax
import jax.numpy as jnp
from jax import lax
from jax.experimental import pallas as pl
from jax.experimental.pallas import tpu as pltpu
from jax.sharding import Mesh
from jax.sharding import PartitionSpec as P

H = 16
DN = 128
DR = 64
DV = 128
KVL = 512
SHARED = 2
EXPERTS = 2

REP = ("zh", "y", "core")
SHARD = ("x", "zl")

norm_eps = 1e-06
rope_base = 10000.0
masked_score = -1e30
f32 = jnp.float32
bf16 = jnp.bfloat16


def norm_parts(values):
    inverse = lax.rsqrt(jnp.mean(values * values, axis=-1, keepdims=True) + norm_eps)
    return (values * inverse, inverse)


def norm_back(grad_normed, normed, inverse):
    return inverse * (grad_normed - normed * jnp.mean(grad_normed * normed, axis=-1, keepdims=True))


def rotary_tables(places, width):
    half_width = width // 2
    inverse = jnp.exp(-jnp.log(rope_base) * (2.0 * jnp.arange(half_width, dtype=f32) / width))
    turns = places.astype(f32)[:, None] * inverse[None, :]
    cosine = jnp.cos(turns)
    sine_tab = jnp.sin(turns)
    return (jnp.concatenate([cosine, cosine], -1), jnp.concatenate([sine_tab, sine_tab], -1))


def dot(a, b, dims):
    return lax.dot_general(a, b, ((dims[:1], dims[1:]), ((), ())), preferred_element_type=f32)


def right(v):
    size = lax.axis_size("x")
    return lax.ppermute(v, "x", [(i, (i + 1) % size) for i in range(size)])


def left(v):
    size = lax.axis_size("x")
    return lax.ppermute(v, "x", [(i, (i - 1) % size) for i in range(size)])


def flip(v):
    return lax.ppermute(v, "zl", [(0, 1), (1, 0)])


def to_relative(v):
    v = v.reshape((4, 2) + v.shape[1:])
    v = lax.dynamic_slice_in_dim(jnp.concatenate([v, v], 0), lax.axis_index("x"), 4, 0)
    v = jnp.where(lax.axis_index("zl") == 0, v, v[:, ::-1])
    v = jnp.swapaxes(v.reshape((4, 2, 2, v.shape[2] // 2) + v.shape[3:]), 1, 2)
    return v.reshape((-1,) + v.shape[4:])


def whole_first(v):
    return {(0, 0): v, (3, 0): right(v), (0, 1): flip(v), (1, 0): left(v)}


def whole_second(got):
    more = {(2, 0): right(got[3, 0]), (3, 1): flip(got[3, 0]), (1, 1): left(got[0, 1])}
    return {**got, **more}


def whole_third(got):
    return {**got, (2, 1): left(got[1, 1])}


def gather_pairs(v, tie=None, first=(), last=None):
    other, before, after, _ = lax.optimization_barrier((flip(v), right(v), left(v), first))
    got = {(0, 0): v, (0, 1): other, (3, 0): before, (1, 0): after}
    got[2, 0] = right(before)
    got[3, 1], got[1, 1] = right(other), left(other)
    if tie is not None:
        got[2, 0], tie = lax.optimization_barrier((got[2, 0], tie))
    got[2, 1] = left(got[1, 1])
    if last is not None:
        got[2, 1], tie = lax.optimization_barrier((got[2, 1], last(tie)))
    got = [(got[x, z], ((x, 0, z), (x, 1, z))) for z in range(2) for x in range(4)]
    return got if tie is None else (got, tie)


def scatter_parts(v):
    unit = v.shape[0] // 8
    return {(x, h): v[(2 * x + h) * unit : (2 * x + h + 1) * unit] for x in range(4) for h in range(2)}


def scatter_sends(part):
    return (left(part[2, 0]), right(part[2, 1]), right(part[1, 0]), left(part[3, 1]))


def scatter_first(v):
    part = scatter_parts(v)
    return part, scatter_sends(part)


def scatter_second(part, sent):
    far_a, far_b, near_a, near_b = sent
    low = add(part[3, 0], far_a).astype(bf16)
    high = add(part[1, 1], far_b).astype(bf16)
    low, high = lax.optimization_barrier((low, high))
    return (part[0, 0], part[0, 1], near_a, near_b), (left(low), right(high))


def scatter_third(own, sent):
    half = own[0].shape[0] // 2
    a = add(own[0], own[2], sent[0])
    b = add(own[1], own[3], sent[1])
    other = flip(jnp.concatenate([a[half:], b[half:]], 0).astype(bf16))
    return jnp.concatenate([a[:half], b[:half]], 0), other


def merged_rows(v, works=((), (), ())):
    tie = lax.optimization_barrier
    done = []

    def beside(n, sent):
        if works[n]:
            sent, got = tie((sent, works[n](done)))
            done.append(got)
        return sent

    part, sent = scatter_first(v)
    half = part[0, 0].shape[0] // 2
    far, near = sent[:2], sent[2:]
    far = beside(0, far)
    low, high = add(part[3, 0], far[0]), add(part[1, 1], far[1])
    side = flip(jnp.concatenate([low[half:], high[half:]], 0).astype(bf16))
    low, high = low[:half].astype(bf16), high[:half].astype(bf16)
    side, near = beside(1, tie((side, near)))
    low = add(low, side[:half]).astype(bf16)
    high = add(high, side[half:]).astype(bf16)
    own_a, own_b = add(part[0, 0], near[0]), add(part[0, 1], near[1])
    across = jnp.concatenate([own_a[half:], own_b[half:]], 0).astype(bf16)
    low, high, across = tie((low, high, across))
    last = beside(2, (flip(across), left(low), right(high)))
    own = jnp.concatenate([own_a[:half], own_b[:half]], 0)
    out = add(own, last[0], jnp.concatenate(last[1:], 0))
    return (out, *done) if done else out


def add(*terms):
    return sum(t.astype(f32) for t in terms)


def swap(v):
    return lax.ppermute(v, "core", [(0, 1), (1, 0)])


def hop(v):
    return lax.ppermute(v, "zh", [(0, 1), (1, 0)])


def up(v):
    size = lax.axis_size("y")
    return lax.ppermute(v, "y", [(i, (i + 1) % size) for i in range(size)])


def down(v):
    size = lax.axis_size("y")
    return lax.ppermute(v, "y", [(i, (i - 1) % size) for i in range(size)])


def pick(v, index, axis):
    return lax.dynamic_index_in_dim(v, index, axis, keepdims=False)


def ring_gather(v):
    if lax.axis_size("y") == 1:
        return [(0, 0, v)]
    half = v.shape[0] // 2
    before, after = up(v), down(v)
    across = up(before[:half]), down(after[half:])
    return [(0, 0, v), (1, 0, after), (3, 0, before), (2, 0, across[0]), (2, half, across[1])]


def ring_first(p):
    if len(p) == 1:
        return ()
    half = p[0].shape[0] // 2
    return (down(p[2][:half]), up(p[2][half:]))


def ring_second(p, sent):
    if len(p) == 1:
        return (p[0],)
    half = p[0].shape[0] // 2
    low = jnp.concatenate([add(p[3][:half], sent[0]).astype(bf16), p[3][half:]], 0)
    high = jnp.concatenate([p[1][:half], add(p[1][half:], sent[1]).astype(bf16)], 0)
    return (p[0], down(low), up(high))


def rep_gather(v):
    zh = lax.axis_index("zh")
    highs, cores = lax.axis_size("zh"), lax.axis_size("core")
    pair = v
    if highs > 1:
        other = hop(v)
        pair = jnp.where(zh == 0, jnp.concatenate([v, other], 0), jnp.concatenate([other, v], 0))
    pieces = []
    for block in ring_gather(pair):
        pieces += [block, swap(block)] if cores > 1 else [block]
    return pieces


def scatter_rows(v, tie=None):
    part, sent = scatter_first(v)
    if tie is not None:
        sent, tie = lax.optimization_barrier((sent, tie))
    out = add(*scatter_third(*scatter_second(part, sent)))
    return out if tie is None else (out, tie)


MIB = 1 << 20
VM = pl.BlockSpec(memory_space=pltpu.VMEM)
SM = pl.BlockSpec(memory_space=pltpu.SMEM)


def on_core(kernel, outs, in_specs, flops, byts, scratch=(), **more):
    return pl.pallas_call(
        kernel,
        out_shape=outs,
        in_specs=in_specs,
        out_specs=jax.tree.map(lambda _: VM, outs),
        scratch_shapes=list(scratch),
        compiler_params=pltpu.CompilerParams(vmem_limit_bytes=56 * MIB),
        cost_estimate=pl.CostEstimate(flops=flops, bytes_accessed=byts, transcendentals=0),
        **more,
    )


def chunk_kernel(at_ref, query_ref, down_ref, up_ref, row_ref, out_ref, *, sub, qw, kvw):
    begin = pl.multiple_of(at_ref[4], sub)
    piece = min(sub, up_ref.shape[0])
    query = query_ref[pl.ds(begin, sub), :]
    down = down_ref[pl.ds(begin, sub), :]
    parts = out_ref.shape[0]
    lanes = 128
    cols = up_ref.shape[1] // parts
    shared = jnp.concatenate([down, down[:, kvw - DR :]], 1)
    row = jnp.broadcast_to(row_ref[...], (out_ref.shape[1] - sub, out_ref.shape[2]))
    for d in range(parts):
        out_ref[d, :sub, :qw] = query[:, d * qw : (d + 1) * qw]
        out_ref[d, :sub, qw : qw + kvw + DR] = shared
        out_ref[d, sub:, :] = row
    for k in range(sub // piece):
        spot = begin + k * piece
        group = spot // up_ref.shape[0]
        first = pl.multiple_of(lax.rem(spot, up_ref.shape[0]), piece)
        for d in range(parts):
            col = pl.multiple_of(d * cols + group * lanes, lanes)
            out_ref[d, k * piece : (k + 1) * piece, qw + kvw + DR :] = up_ref[
                pl.ds(first, piece), pl.ds(col, lanes)
            ]


def weights_kernel(at_ref, *refs, places, cores, sub, spots):
    blocks, (cat_ref, up_ref) = refs[: len(spots)], refs[len(spots) :]
    y, core = at_ref[2], at_ref[3]
    parts = max(low + ref.shape[0] for ref, (_, low, _) in zip(blocks, spots))
    d_rows = cat_ref.shape[0] // parts
    kv_rows = up_ref.shape[0] // parts
    cat = cat_ref.shape[1]
    piece = min(sub, kv_rows)
    for ref, (step, low_d, n) in zip(blocks, spots):
        spot = lax.rem(y + step, places) * cores
        first = (spot + (core if n == 0 else 1 - core)) * sub
        for k_d in range(ref.shape[0]):
            d = low_d + k_d
            cat_ref[pl.ds(pl.multiple_of(d * d_rows + first, sub), sub), :] = ref[k_d, :sub, :cat]
            for k in range(sub // piece):
                row = first + k * piece
                low = pl.multiple_of(d * kv_rows + lax.rem(row, kv_rows), piece)
                col = pl.multiple_of(row // kv_rows * 128, 128)
                up_ref[pl.ds(low, piece), pl.ds(col, 128)] = ref[
                    k_d, k * piece : (k + 1) * piece, cat:
                ]


def norm_kernel(gain_ref, *refs, spots):
    blocks, out_ref = refs[:-1], refs[-1]
    half = out_ref.shape[0] // 16
    step = 16
    gain = gain_ref[...]
    for ref, where in zip(blocks, spots):
        for n, spot in enumerate(where):

            def body(i, carry):
                row = pl.multiple_of(i * step, step)
                values = ref[pl.ds(n * half + row, step), :].astype(f32)
                inverse = lax.rsqrt(jnp.mean(values * values, axis=-1, keepdims=True) + norm_eps)
                out_ref[pl.ds(spot * half + row, step), :] = (values * inverse * gain).astype(bf16)
                return carry

            lax.fori_loop(0, half // step, body, 0, unroll=4)


def assemble_kernel(*refs, spots):
    blocks, out_ref = refs[:-1], refs[-1]
    half = out_ref.shape[0] // 16
    for ref, where in zip(blocks, spots):
        for n, spot in enumerate(where):
            out_ref[spot * half : (spot + 1) * half, :] = ref[n * half : (n + 1) * half, :]


def spots_of(blocks):
    return [[(2 * x + h) * 2 + z for x, h, z in where] for _, where in blocks]


def assemble(blocks):
    width = blocks[0][0].shape[1]
    rows = 8 * blocks[0][0].shape[0]
    kernel = functools.partial(assemble_kernel, spots=spots_of(blocks))
    out = jax.ShapeDtypeStruct((rows, width), bf16)
    return on_core(kernel, out, [VM] * len(blocks), 0, 4 * rows * width)(*[v for v, _ in blocks])


def spots(at_ref, low):
    size = SPAN // 4
    base = lax.rem(low // SPAN - at_ref[0] + 4, 4) * SPAN
    for z in range(2):
        other = at_ref[1] if z == 0 else 1 - at_ref[1]
        for h in range(2):
            yield pl.ds(pl.multiple_of(base + h * 2 * size + other * size, size), size)


def read_rows(at_ref, ref, low, cols):
    return jnp.concatenate([ref[spot, cols] for spot in spots(at_ref, low)], 0)


def write_rows(at_ref, ref, low, cols, value):
    size = SPAN // 4
    for n, spot in enumerate(spots(at_ref, low)):
        ref[spot, cols] = value[n * size : (n + 1) * size]


def turn_lanes(v):
    lane = lax.broadcasted_iota(jnp.int32, v.shape, 1) % DR
    return jnp.where(lane < DR // 2, -pltpu.roll(v, 128 - DR // 2, 1), pltpu.roll(v, DR // 2, 1))


def head_mask(shape, h):
    lane = lax.broadcasted_iota(jnp.int32, shape, 1)
    return lane >= DR if h == 0 else lane < DR


SPAN = 256
SCALE = (DN + DR) ** (-0.5)


def head_query(q_ref, h, low):
    rope = q_ref[low : low + SPAN, 2 * DN : 2 * DN + 128]
    rope = jnp.where(head_mask(rope.shape, h), rope, jnp.zeros_like(rope))
    return jnp.concatenate([q_ref[low : low + SPAN, h * DN : (h + 1) * DN], rope], 1)


def head_keys(kv_ref, kr_ref, h, count):
    return jnp.concatenate([kv_ref[:count, h * 256 : h * 256 + DN], kr_ref[:count, :]], 1)


def allowed_block(idc_ref, idr_ref, low, count):
    row = lax.broadcasted_iota(jnp.int32, (SPAN, count), 0) + low
    col = lax.broadcasted_iota(jnp.int32, (SPAN, count), 1)
    return (col <= row) & (idc_ref[low : low + SPAN, :] == idr_ref[:, :count])


def forward_kernel(
    at_ref, pre_ref, gain_ref, up_ref, cos_ref, sin_ref, idc_ref, idr_ref,
    q_ref, lat_ref, kv_ref, kr_ref, lse_ref, ctx_ref,
):
    length = pre_ref.shape[0]
    for low in range(0, length, SPAN):
        rows = slice(low, low + SPAN)
        cosine, sine = cos_ref[rows, :], sin_ref[rows, :]
        pre = read_rows(at_ref, pre_ref, low, slice(None))
        mid = pltpu.roll(pre[:, DN : DN + 256], 256 - DR, 1)
        rope = mid[:, 128:]
        q_ref[rows, :DN] = pre[:, :DN].astype(bf16)
        q_ref[rows, DN : 2 * DN] = mid[:, :DN].astype(bf16)
        q_ref[rows, 2 * DN :] = (rope * cosine + turn_lanes(rope) * sine).astype(bf16)
        lat = pre[:, 384 : 384 + KVL]
        inverse = lax.rsqrt(jnp.mean(lat * lat, axis=-1, keepdims=True) + norm_eps)
        latent = (lat * inverse * gain_ref[...]).astype(bf16)
        lat_ref[rows, :] = latent
        rope = pre[:, 384 + KVL :]
        kr_ref[rows, :] = (rope * cosine + turn_lanes(rope) * sine).astype(bf16)
        kv_ref[rows, :] = dot(latent, up_ref[...], (1, 0)).astype(bf16)
    for low in range(0, length, SPAN):
        count = low + SPAN
        allowed = allowed_block(idc_ref, idr_ref, low, count)
        for h in range(2):
            scores = dot(head_query(q_ref, h, low), head_keys(kv_ref, kr_ref, h, count), (1, 1))
            scores = jnp.where(allowed, scores * SCALE, masked_score)
            top = jnp.max(scores, axis=-1, keepdims=True)
            expo = jnp.exp(scores - top)
            total = jnp.sum(expo, axis=-1, keepdims=True)
            lse_ref[h, low:count, :] = jnp.broadcast_to(top + jnp.log(total), (SPAN, 128))
            probs = (expo * (1.0 / total)).astype(bf16)
            values = kv_ref[:count, h * 256 + DN : (h + 1) * 256]
            context = dot(probs, values, (1, 0)).astype(bf16)
            write_rows(at_ref, ctx_ref, low, slice(h * DV, (h + 1) * DV), context)


def backward_kernel(
    at_ref, gctx_ref, q_ref, kv_ref, kr_ref, lse_ref, pre_ref, gain_ref, up_ref, cos_ref, sin_ref,
    idc_ref, idr_ref, gp_ref, gkv_ref, dq_ref, dqr_ref, dk_ref, dv_ref, dkr_ref,
):
    length = gctx_ref.shape[0]
    for h in range(2):
        for low in reversed(range(0, length, SPAN)):
            count = low + SPAN
            allowed = allowed_block(idc_ref, idr_ref, low, count)
            query = head_query(q_ref, h, low)
            keys = head_keys(kv_ref, kr_ref, h, count)
            scores = jnp.where(allowed, dot(query, keys, (1, 1)) * SCALE, masked_score)
            probs = jnp.exp(scores - lse_ref[h, low:count, :1])
            grad_ctx = read_rows(at_ref, gctx_ref, low, slice(h * DV, (h + 1) * DV))
            values = kv_ref[:count, h * 256 + DN : (h + 1) * 256]
            grad_probs = dot(grad_ctx, values, (1, 1))
            row_dot = jnp.sum(probs * grad_probs, axis=-1, keepdims=True)
            grad_scores = (probs * (grad_probs - row_dot)).astype(bf16)
            grad_query = dot(grad_scores, keys, (1, 0))
            dq_ref[low:count, h * DN : (h + 1) * DN] = grad_query[:, :DN]
            rope = jnp.where(head_mask((SPAN, 128), h), grad_query[:, DN:], 0.0)
            dqr_ref[low:count, :] = rope if h == 0 else dqr_ref[low:count, :] + rope
            grad_keys = dot(grad_scores, query, (0, 0))
            grad_values = dot(probs.astype(bf16), grad_ctx, (0, 0))
            if count == length:
                dk_ref[...] = grad_keys
                dv_ref[...] = grad_values
            else:
                dk_ref[:count, :] = dk_ref[:count, :] + grad_keys
                dv_ref[:count, :] = dv_ref[:count, :] + grad_values
        gkv_ref[:, h * 256 : h * 256 + DN] = (dk_ref[:, :DN] * SCALE).astype(bf16)
        gkv_ref[:, h * 256 + DN : (h + 1) * 256] = dv_ref[...].astype(bf16)
        rope = dk_ref[:, DN:]
        dkr_ref[...] = rope if h == 0 else dkr_ref[...] + rope
    for low in range(0, length, SPAN):
        rows = slice(low, low + SPAN)
        cosine, sine = cos_ref[rows, :], sin_ref[rows, :]
        grad_query = (dq_ref[rows, :DN] * SCALE).astype(bf16)
        write_rows(at_ref, gp_ref, low, slice(0, DN), grad_query)
        rope = dqr_ref[rows, :] * SCALE
        rope = rope * cosine - turn_lanes(rope) * sine
        mid = jnp.concatenate([dq_ref[rows, DN : 2 * DN] * SCALE, rope], 1)
        mid = pltpu.roll(mid, DR, 1).astype(bf16)
        write_rows(at_ref, gp_ref, low, slice(DN, DN + 256), mid)
        grad_latent = dot(gkv_ref[rows, :], up_ref[...], (1, 1)) * gain_ref[...]
        lat = read_rows(at_ref, pre_ref, low, slice(384, 384 + KVL))
        inverse = lax.rsqrt(jnp.mean(lat * lat, axis=-1, keepdims=True) + norm_eps)
        normed = lat * inverse
        inner = jnp.mean(grad_latent * normed, axis=-1, keepdims=True)
        grad_latent = (inverse * (grad_latent - normed * inner)).astype(bf16)
        write_rows(at_ref, gp_ref, low, slice(384, 384 + KVL), grad_latent)
        rope = dkr_ref[rows, :]
        rope = (rope + pltpu.roll(rope, DR, 1)) * SCALE
        rope = rope * cosine - turn_lanes(rope) * sine
        rope = jnp.where(head_mask(rope.shape, 1), rope, 0.0).astype(bf16)
        write_rows(at_ref, gp_ref, low, slice(384 + KVL, 512 + KVL), rope)


def sends_kernel(
    at_ref, normed_ref, gp_ref, cat_ref, upp_ref, up_ref, one_ref, kv_ref, two_ref, part_ref,
    *refs, places, cores, parts,
):
    outs, all_ref = refs[:-1], refs[-1]
    d = pl.program_id(0)
    d_rows = all_ref.shape[0]

    @pl.when(d < parts)
    def _():
        part = dot(normed_ref[...], gp_ref[...], (0, 0))
        wide = part.shape[1]
        one = jnp.sum(part * cat_ref[...].astype(f32), axis=-1, keepdims=True) / one_ref[...]
        kv = jnp.sum(upp_ref[...] * up_ref[...].astype(f32), axis=-1, keepdims=True) / kv_ref[...]
        all_ref[:, : wide - 128] = part[:, : wide - 128].astype(bf16)
        count = kv.shape[0]
        lane = lax.broadcasted_iota(jnp.int32, (count, 128), 1)
        for g in range(d_rows // count):
            rows = slice(g * count, (g + 1) * count)
            last = jnp.where(lane < 64, part[rows, wide - 128 :], 0.0)
            last = jnp.where(lane == 64, one[rows, :], last)
            last = jnp.where(lane == 65, two_ref[rows, :], last)
            if g == 0:
                last = jnp.where(lane == 66, kv, last)
            all_ref[rows, wide - 128 : wide] = last.astype(bf16)
            all_ref[rows, wide:] = upp_ref[:, g * 128 : (g + 1) * 128].astype(bf16)

    @pl.when(d >= parts)
    def _():
        all_ref[:, : part_ref.shape[1]] = part_ref[...]

    size = d_rows // (places * cores)
    y, core = at_ref[2], at_ref[3]
    for r in range(places):
        spot = lax.rem(y + r, places) * cores
        for n, ref in enumerate(outs):
            first = (spot + (core if n == 0 else 1 - core)) * size
            ref[r, 0] = all_ref[pl.ds(pl.multiple_of(first, size), size), :]


def expert_pack_kernel(at_ref, *refs, cores):
    parts, outs = refs[:3], refs[3:]
    size = parts[0].shape[0] // cores
    core = at_ref[3]
    for n, out_ref in enumerate(outs):
        first = (core if n == 0 else 1 - core) * size
        rows = pl.ds(pl.multiple_of(first, 16), size)
        for k, ref in enumerate(parts):
            out_ref[0, k * size : (k + 1) * size, :] = ref[rows, :]


def expert_unpack_kernel(at_ref, *refs, cores):
    blocks, outs = refs[:cores], refs[-3:]
    size = blocks[0].shape[0] // 3
    core = at_ref[3]
    for n, ref in enumerate(blocks):
        first = (core if n == 0 else 1 - core) * size
        rows = pl.ds(pl.multiple_of(first, 16), size)
        for k, out_ref in enumerate(outs):
            out_ref[rows, :] = ref[k * size : (k + 1) * size, :].astype(f32)


def expert_pack(at, parts, places, cores):
    rows, width = parts[0].shape
    cols = width // places
    out = jax.ShapeDtypeStruct((places, 3 * rows // cores, cols), bf16)
    return pl.pallas_call(
        functools.partial(expert_pack_kernel, cores=cores),
        out_shape=[out] * cores,
        grid_spec=pltpu.PrefetchScalarGridSpec(
            num_scalar_prefetch=1,
            grid=(places,),
            in_specs=[pl.BlockSpec((rows, cols), lambda r, at: (0, lax.rem(at[2] + r, places)))] * 3,
            out_specs=[pl.BlockSpec((1,) + out.shape[1:], lambda r, at: (r, 0, 0))] * cores,
        ),
        compiler_params=pltpu.CompilerParams(vmem_limit_bytes=40 * MIB),
        cost_estimate=pl.CostEstimate(flops=0, bytes_accessed=16 * MIB, transcendentals=0),
    )(at, *parts)


def expert_unpack(at, step, blocks, held, places, rows, width):
    cores = len(blocks)
    cols = width // places
    out = jax.ShapeDtypeStruct((rows, width), f32)
    held = list(held)
    return pl.pallas_call(
        functools.partial(expert_unpack_kernel, cores=cores),
        out_shape=[out] * 3,
        grid_spec=pltpu.PrefetchScalarGridSpec(
            num_scalar_prefetch=1,
            grid=(1,),
            in_specs=[pl.BlockSpec(blocks[0].shape, lambda i, at: (0, 0))] * cores
            + [pl.BlockSpec(memory_space=pl.ANY)] * len(held),
            out_specs=[pl.BlockSpec((rows, cols), lambda i, at: (0, lax.rem(at[2] + step, places)))] * 3,
        ),
        input_output_aliases={1 + cores + k: k for k in range(len(held))},
        compiler_params=pltpu.CompilerParams(vmem_limit_bytes=40 * MIB),
        cost_estimate=pl.CostEstimate(flops=0, bytes_accessed=6 * MIB, transcendentals=0),
    )(at, *blocks, *held)


def join_kernel(own_ref, part_ref, out_ref, *, qw, cat):
    parts = own_ref.shape[0]
    mid = parts * qw
    end = mid + cat - qw
    total = jnp.zeros((own_ref.shape[1], cat - qw), f32)
    for d in range(parts):
        out_ref[:, d * qw : (d + 1) * qw] = own_ref[d, :, :qw]
        total = total + own_ref[d, :, qw:cat].astype(f32)
        out_ref[:, end + d * 128 : end + (d + 1) * 128] = own_ref[d, :, cat:]
    out_ref[:, mid:end] = total.astype(bf16)
    first = end + parts * 128
    for n in range(part_ref.shape[0]):
        out_ref[:, first + n * cat : first + (n + 1) * cat] = part_ref[n, :, :cat]


def unpack_kernel(at_ref, *refs, places, cores, size, parts):
    blocks, outs = refs[: places * cores], refs[places * cores :]
    query_ref, down_ref, one_ref, two_ref, kv_ref, up_ref, out_ref, mid_ref = outs
    qw, kvw = query_ref.shape[1], down_ref.shape[0]
    kv_rows = up_ref.shape[0]
    kv_cols = up_ref.shape[1] // parts
    mid = qw + kvw + 64
    piece = min(size, kv_rows)
    y, core = at_ref[2], at_ref[3]
    for n, ref in enumerate(blocks):
        spot = lax.rem(y + n // cores, places) * cores
        spot = spot + (core if n % cores == 0 else 1 - core)
        first = pl.multiple_of(spot * size, size)
        rows = pl.ds(first, size)
        query_ref[rows, :] = ref[:, :qw].astype(f32)
        mid_ref[rows, :] = ref[:, qw:mid].astype(f32)
        out_ref[rows, :] = ref[:, mid + parts * 128 :].astype(f32)
        for k in range(size // piece):
            row = first + k * piece
            low = pl.multiple_of(lax.rem(row, kv_rows), piece)
            for d in range(parts):
                col = pl.multiple_of(d * kv_cols + row // kv_rows * 128, 128)
                value = ref[k * piece : (k + 1) * piece, mid + d * 128 : mid + (d + 1) * 128]
                up_ref[pl.ds(low, piece), pl.ds(col, 128)] = value.astype(f32)
    cols = mid_ref[...].T
    down_ref[...] = cols[:kvw, :]
    one_ref[...] = cols[kvw : kvw + 1, :]
    two_ref[...] = cols[kvw + 1 : kvw + 2, :]
    kv_ref[...] = cols[kvw + 2 : kvw + 3, :kv_rows]


def local(
    tokens,
    segments,
    routes,
    gate_scores,
    attn_gain,
    w_query,
    w_down_kv,
    kv_gain,
    w_up_kv,
    w_out,
    ffn_gain,
    w_gate,
    w_up,
    w_down,
    cotangent,
):
    parts = lax.axis_size(SHARD)
    rows, width = tokens.shape
    length = rows * parts
    experts, _, units = w_gate.shape
    d_rows, kvw = w_down_kv.shape
    qw = w_query.shape[1] // parts
    kv_rows, kv_cols = w_up_kv.shape[0], w_up_kv.shape[1] // parts
    zh, y, core = (lax.axis_index(name) for name in REP)
    highs, places, cores = (lax.axis_size(name) for name in REP)
    sub = d_rows // (places * cores)
    at = jnp.stack(
        [lax.axis_index("x"), lax.axis_index("zl"), y, core, (y * cores + core) * sub]
    ).astype(jnp.int32)
    ids = lax.dynamic_slice_in_dim(segments, lax.axis_index(REP) * length, length)
    cosine, sine_tab = rotary_tables(jnp.arange(length, dtype=jnp.int32), DR)
    cosine = jnp.concatenate([cosine, cosine], 1)
    sine_tab = jnp.concatenate([sine_tab, sine_tab], 1)

    chosen = routes[:, :, None] == jnp.arange(EXPERTS, dtype=jnp.int32)[None, None, :]
    routed = jnp.sum(jnp.where(chosen, gate_scores.astype(f32)[:, :, None], 0.0), axis=1)
    cat = qw + kvw + DR
    wide = cat + 128
    tail = [attn_gain, ffn_gain, routed.astype(bf16).reshape(-1), kv_gain]
    row = jnp.concatenate(tail)
    row = jnp.pad(row, (0, wide - row.shape[0]))[None, :]
    chunk = on_core(
        functools.partial(chunk_kernel, sub=sub, qw=qw, kvw=kvw),
        jax.ShapeDtypeStruct((parts, sub + 16, wide), bf16),
        [SM] + [VM] * 4,
        0,
        4 * MIB,
    )(at, w_query, w_down_kv, w_up_kv, row)
    chunk = lax.all_to_all(chunk, SHARD, split_axis=0, concat_axis=0, tiled=True)
    ring = ring_gather(chunk[:, :sub])
    blocks = gather_pairs(tokens, first=chunk)
    pieces, places_of = [], []
    for step, low, block in ring:
        pieces += [block, swap(block)] if cores > 1 else [block]
        places_of += [(step, low, n) for n in range(cores)]
    held, late = lax.optimization_barrier((blocks[2][0], cotangent))
    blocks[2] = (held, blocks[2][1])
    cot = whole_third(whole_second(whole_first(late)))
    cat_w, up_kv_w = on_core(
        functools.partial(weights_kernel, places=places, cores=cores, sub=sub, spots=places_of),
        (
            jax.ShapeDtypeStruct((parts * d_rows, cat), bf16),
            jax.ShapeDtypeStruct((parts * kv_rows, kv_cols), bf16),
        ),
        [SM] + [VM] * len(pieces),
        0,
        10 * MIB,
    )(at, *pieces)
    tail_rows = chunk[:, sub].astype(f32)
    ends = [d_rows, 2 * d_rows, 2 * d_rows + rows * EXPERTS]
    gain_one = tail_rows[:, : ends[0]].reshape(1, -1)
    gain_two = tail_rows[:, ends[0] : ends[1]].reshape(1, -1)
    routed_all = to_relative(tail_rows[:, ends[1] : ends[2]].reshape(parts, rows, EXPERTS))
    gain_kv = tail_rows[:, ends[2] : ends[2] + kv_rows].reshape(1, -1)

    normed = on_core(
        functools.partial(norm_kernel, spots=spots_of(blocks)),
        jax.ShapeDtypeStruct((length, width), bf16),
        [VM] * (1 + len(blocks)),
        0,
        8 * MIB,
    )(gain_one, *[v for v, _ in blocks])
    pre = dot(normed, cat_w, (1, 0))
    shape = jax.ShapeDtypeStruct
    queries, latent, key_value, key_rope, log_total, context = on_core(
        forward_kernel,
        (
            shape((length, qw), bf16),
            shape((length, KVL), bf16),
            shape((length, kv_cols), bf16),
            shape((length, 128), bf16),
            shape((2, length, 128), f32),
            shape((length, 2 * DV), bf16),
        ),
        [SM] + [VM] * 7,
        0,
        10 * MIB,
    )(at, pre, gain_kv, up_kv_w, cosine, sine_tab, ids[:, None], ids[None, :])
    context, cot = lax.optimization_barrier((context, cot))
    grad_out_all = assemble([(v, ((x, 0, z), (x, 1, z))) for (x, z), v in cot.items()])
    inputs_f = tokens.astype(f32)
    residual = inputs_f + merged_rows(dot(context, w_out, (1, 0)).astype(bf16))
    normed_two, inverse_two = norm_parts(residual)
    ffn_own = (normed_two * gain_two).astype(bf16)
    ffn_in = assemble(gather_pairs(ffn_own))

    gate_t = jnp.swapaxes(w_gate, 1, 2).reshape(experts * units, width)
    up_t = jnp.swapaxes(w_up, 1, 2).reshape(experts * units, width)
    down_t = w_down.reshape(experts * units, width)
    expert_of = (jnp.arange(experts * units, dtype=jnp.int32) // units)[None, :]
    weight_cols = jnp.ones((length, experts * units), f32)
    for m in range(EXPERTS):
        weight_cols = jnp.where(expert_of == SHARED + m, routed_all[:, m : m + 1], weight_cols)
    gate_pre = dot(ffn_in, gate_t, (1, 1))
    up_pre = dot(ffn_in, up_t, (1, 1))
    sig = jax.nn.sigmoid(gate_pre)
    hidden = (gate_pre * sig * up_pre * weight_cols).astype(bf16)
    grad_hidden = dot(grad_out_all, down_t, (1, 1))
    scaled = grad_hidden * weight_cols
    grad_gate = (scaled * up_pre * sig * (1.0 + gate_pre * (1.0 - sig))).astype(bf16)
    grad_up = (scaled * gate_pre * sig).astype(bf16)
    grad_ffn = (dot(grad_gate, gate_t, (1, 0)) + dot(grad_up, up_t, (1, 0))).astype(bf16)
    grad_ffn, hidden, grad_gate, grad_up = lax.optimization_barrier(
        (grad_ffn, hidden, grad_gate, grad_up)
    )
    ffn_part = dot(hidden, down_t, (1, 0)).astype(bf16)
    tie = lax.optimization_barrier

    def products(found):
        _, gate, up_ = tie((found[0], grad_gate, grad_up))
        return dot(gate, ffn_in, (0, 0)).astype(bf16), dot(up_, ffn_in, (0, 0)).astype(bf16)

    def packed(found):
        down_part, (gate_part, up_part) = found
        return expert_pack(at, (gate_part, up_part, down_part), places, cores)

    grad_ffn, _, _, (ex_own, *ex_other) = merged_rows(
        grad_ffn,
        (
            lambda found: dot(hidden, grad_out_all, (0, 0)).astype(bf16),
            products,
            packed,
        ),
    )
    ex_got = [swap(v) for v in ex_other]
    gain_two_part = jnp.sum(grad_ffn * normed_two, axis=0)
    grad_residual = cotangent.astype(f32) + norm_back(grad_ffn * gain_two, normed_two, inverse_two)
    blocks, (ex_own, out_parts) = gather_pairs(
        grad_residual.astype(bf16),
        ex_got,
        ffn_part,
        lambda got: (add(ex_own, *got).astype(bf16), scatter_parts(ffn_part)),
    )
    ex_own = [ex_own[r] for r in range(places)]
    ex_got = ring_first(ex_own)
    grad_branch = assemble(blocks)
    grad_branch, out_parts = tie((grad_branch, out_parts))
    out_sent = scatter_sends(out_parts)

    out_part = dot(context, grad_branch, (0, 0)).astype(bf16)
    grad_context = dot(grad_branch, w_out, (1, 1)).astype(bf16)
    grad_pre, grad_key_value = on_core(
        backward_kernel,
        (shape((length, cat), bf16), shape((length, kv_cols), bf16)),
        [SM] + [VM] * 12,
        0,
        15 * MIB,
        [
            pltpu.VMEM((length, 2 * DN), f32),
            pltpu.VMEM((length, 128), f32),
            pltpu.VMEM((length, 256), f32),
            pltpu.VMEM((length, DV), f32),
            pltpu.VMEM((length, 128), f32),
        ],
    )(
        at, grad_context, queries, key_value, key_rope, log_total, pre, gain_kv, up_kv_w,
        cosine, sine_tab, ids[:, None], ids[None, :],
    )
    grad_pre, ex_got, out_sent = tie((grad_pre, ex_got, out_sent))
    ex_own = ring_second(ex_own, ex_got)
    up_kv_part = dot(latent, grad_key_value, (0, 0))
    size = d_rows // (places * cores)
    slabs = width // cat
    last = parts - 1
    sends = pl.pallas_call(
        functools.partial(sends_kernel, places=places, cores=cores, parts=parts),
        out_shape=[shape((places, parts + slabs, size, wide), bf16)] * cores,
        grid=(parts + slabs,),
        in_specs=[
            SM,
            pl.BlockSpec((length, d_rows), lambda d: (0, jnp.minimum(d, last))),
            pl.BlockSpec((length, cat), lambda d: (0, 0)),
            pl.BlockSpec((d_rows, cat), lambda d: (jnp.minimum(d, last), 0)),
            pl.BlockSpec((kv_rows, kv_cols), lambda d: (jnp.minimum(d, last), 0)),
            pl.BlockSpec((kv_rows, kv_cols), lambda d: (jnp.minimum(d, last), 0)),
            pl.BlockSpec((d_rows, 1), lambda d: (jnp.minimum(d, last), 0)),
            pl.BlockSpec((kv_rows, 1), lambda d: (jnp.minimum(d, last), 0)),
            pl.BlockSpec((d_rows, 1), lambda d: (jnp.minimum(d, last), 0)),
            pl.BlockSpec((d_rows, cat), lambda d: (0, jnp.maximum(d - parts, 0))),
        ],
        out_specs=[pl.BlockSpec((places, 1, size, wide), lambda d: (0, d, 0, 0))] * cores,
        scratch_shapes=[pltpu.VMEM((d_rows, wide), bf16)],
        compiler_params=pltpu.CompilerParams(vmem_limit_bytes=40 * MIB),
        cost_estimate=pl.CostEstimate(flops=0, bytes_accessed=16 * MIB, transcendentals=0),
    )(
        at, normed, grad_pre, cat_w, up_kv_part, up_kv_w,
        gain_one.reshape(-1, 1), gain_kv.reshape(-1, 1), gain_two_part.reshape(-1, 1), out_part,
    )
    sends, out_sent, ex_own = tie((sends, out_sent, ex_own))
    own, *other = sends
    got = [swap(v) for v in other]
    ex_own = add(*ex_own).astype(bf16)
    ex_got = ex_own
    if highs > 1:
        ex_own = ex_own.reshape(highs, -1, ex_own.shape[1])
        ex_got = hop(pick(ex_own, 1 - zh, 0))
        ex_own = pick(ex_own, zh, 0)
    out_sent = scatter_second(out_parts, out_sent)
    normed_part = dot(grad_pre, cat_w, (1, 1)).astype(bf16)
    x_parts, x_sent = scatter_first(normed_part)
    got, ex_got = tie((got, ex_got))
    own = add(own, *got).astype(bf16)
    own = [own[r] for r in range(places)]
    got = ring_first(own)
    if highs > 1:
        ex_own = add(ex_own, ex_got).astype(bf16)
        ex_got = hop(ex_own)
    got, out_sent = tie((got, out_sent))
    own = ring_second(own, got)
    out_sent = scatter_third(*out_sent)
    own, ex_got = tie((own, ex_got))
    if highs > 1:
        low = jnp.where(zh == 0, ex_own, ex_got)
        ex_own = jnp.concatenate([low, jnp.where(zh == 0, ex_got, ex_own)], 0)
    pairs = {0: [swap(ex_own)] if cores > 1 else []}
    own = add(*own).astype(bf16)
    got = own
    if highs > 1:
        own = own.reshape(parts + slabs, highs, size // highs, wide)
        got = hop(pick(own, 1 - zh, 1))
        own = pick(own, zh, 1)
    ring = {0: ex_own}
    if places > 1:
        ring[3], ring[1] = up(ex_own), down(ex_own)
    got, x_sent, out_sent = tie((got, x_sent, out_sent))
    if highs > 1:
        own = add(own, got).astype(bf16)
    x_sent = scatter_second(x_parts, x_sent)
    out_own = own[parts:]
    own = lax.all_to_all(own[:parts], SHARD, split_axis=0, concat_axis=0, tiled=True)
    own, out_own, ring, pairs, x_sent = tie((own, out_own, ring, pairs, x_sent))
    own = on_core(
        functools.partial(join_kernel, qw=qw, cat=cat),
        shape((own.shape[1], parts * (qw + 128) + cat - qw + slabs * cat), bf16),
        [VM, VM],
        0,
        MIB,
    )(own, out_own)
    own, ring = tie((own, ring))
    pair = own
    if highs > 1:
        got = hop(own)
    output = (residual + add(*out_sent)).astype(bf16)
    if places > 1:
        half = ring[0].shape[0] // 2
        ring[2] = (up(ring[3][:half]), down(ring[1][half:]))
    for r in (1, 3) if places > 1 else ():
        pairs[r] = [swap(ring[r])] if cores > 1 else []
    if highs > 1:
        got, ring, pairs = tie((got, ring, pairs))
        pair = jnp.where(zh == 0, jnp.concatenate([own, got], 0), jnp.concatenate([got, own], 0))
    x_sent = scatter_third(*x_sent)
    grads = expert_unpack(at, 0, [ex_own, *pairs[0]], (), places, experts * units, width)
    whole = {0: pair}

    def input_grad(sent):
        own_one, inverse_one = norm_parts(inputs_f)
        return grad_residual + norm_back(add(*sent) * gain_one, own_one, inverse_one)

    if places == 1:
        tokens_grad = input_grad(x_sent)
    if places > 1:
        whole[3], whole[1] = up(pair), down(pair)
        ring[2] = jnp.concatenate(ring[2], 0)
        pairs[2] = [swap(ring[2])] if cores > 1 else []
        for r in (1, 3):
            grads = expert_unpack(at, r, [ring[r], *pairs[r]], grads, places, experts * units, width)
        whole, grads, pairs, x_sent = tie((whole, grads, pairs, x_sent))
        half = pair.shape[0] // 2
        across = (up(whole[3][:half]), down(whole[1][half:]))
        tokens_grad = input_grad(x_sent)
        grads = expert_unpack(at, 2, [ring[2], *pairs[2]], grads, places, experts * units, width)
        across, grads, tokens_grad = tie((across, grads, tokens_grad))
        whole[2] = jnp.concatenate(across, 0)
    pieces = []
    for r in range(places):
        pieces += [whole[r], swap(whole[r])] if cores > 1 else [whole[r]]
    gate_sum, up_sum, down_sum = [v.reshape(experts, units, width) for v in grads]
    query_sum, down_kv_sum, one_sum, two_sum, kv_sum, up_kv_sum, out_sum = on_core(
        functools.partial(unpack_kernel, places=places, cores=cores, size=size, parts=parts),
        (
            shape((d_rows, parts * qw), f32),
            shape((kvw, d_rows), f32),
            shape((1, d_rows), f32),
            shape((1, d_rows), f32),
            shape((1, kv_rows), f32),
            shape((kv_rows, parts * kv_cols), f32),
            shape((d_rows, width), f32),
        ),
        [SM] + [VM] * (places * cores),
        0,
        12 * MIB,
        [pltpu.VMEM((d_rows, kvw + DR), f32)],
    )(at, *pieces)
    return (
        output,
        tokens_grad,
        one_sum.reshape(-1),
        query_sum,
        down_kv_sum.T,
        kv_sum.reshape(-1),
        up_kv_sum,
        out_sum,
        two_sum.reshape(-1),
        jnp.swapaxes(gate_sum, 1, 2),
        jnp.swapaxes(up_sum, 1, 2),
        down_sum,
    )


def split_mesh(mesh):
    reps = mesh.shape["rep"]
    shards = mesh.shape["shard"]
    zh, core = (2, 2) if reps % 4 == 0 else (1, 1)
    zl = 2 if shards % 2 == 0 else 1
    shape = (zh, reps // (zh * core), core, shards // zl, zl)
    return Mesh(mesh.devices.reshape(shape), REP + SHARD)


def solution(mesh):
    every = REP + SHARD
    in_specs = (
        P(every, None),
        P(),
        P(every, None),
        P(every, None),
        P(SHARD),
        P(SHARD, None),
        P(SHARD, None),
        P(SHARD),
        P(SHARD, None),
        P(SHARD, None),
        P(SHARD),
        P(None, None, SHARD),
        P(None, None, SHARD),
        P(None, SHARD, None),
        P(every, None),
    )
    out_specs = (
        P(every, None),
        P(every, None),
        P(SHARD),
        P(SHARD, None),
        P(SHARD, None),
        P(SHARD),
        P(SHARD, None),
        P(SHARD, None),
        P(SHARD),
        P(None, None, SHARD),
        P(None, None, SHARD),
        P(None, SHARD, None),
    )
    return jax.shard_map(
        local, mesh=split_mesh(mesh), in_specs=in_specs, out_specs=out_specs, check_vma=False
    )
```

time: 4530 us -> 546 us (0.12)
  waiting for transfers between devices: 4060 us -> 192 us
  blocking collectives: 147 us -> 0 us
  matrix products: 208 us -> 62.1 us
  starting transfers between devices: 1.36 us -> 135 us
  Pallas kernels: 0 us -> 82.4 us
    all_gather x8 -> x0, waiting for transfers between devices: 1920 us -> none  [the longest x1 445 us: ffn_weights(): lax.all_gather(w_up, 'shard', axis=2, tiled=True)]
    reduce_scatter x7 -> x0, waiting for transfers between devices: 1860 us -> none  [the longest x1 448 us: local(): lax.psum_scatter(gate_full.astype(jnp.bfloat16), 'shard', scatter_dimensi...]
    ppermute x0 -> x97, waiting for transfers between devices: none -> 187 us  [the longest x24 56.3 us: left(): return lax.ppermute(v, 'x', [(i, (i - 1) % size) for i in range(size)])]
    unnamed x20 -> x0, waiting for transfers between devices: 185 us -> none
    dot_general x30 -> x15, matrix products: 208 us -> 62.1 us  [dot(): lax.dot_general(a, b, ((dims[:1], dims[1:]), ((), ())), preferred_element...]
    ppermute x0 -> x97, starting transfers between devices: none -> 125 us  [the longest x24 50.1 us: left(): return lax.ppermute(v, 'x', [(i, (i - 1) % size) for i in range(size)])]
    psum x1 -> x0, waiting for transfers between devices: 99.3 us -> none  [local(): lax.psum(query_grad.astype(jnp.bfloat16), 'rep').astype(jnp.float32)]
    pallas_call x0 -> x16, Pallas kernels: none -> 82.4 us  [the longest x3 13.2 us: assemble(): on_core(kernel, out, [VM] * len(blocks), 0, 4 * rows * width)]
  transfers between devices with their start and end apart: 18 -> 99, of which waited for: 18 -> 47; matrix products, arithmetic and copies ran while one was open for 5% -> 14% of each run, Pallas kernels for 0% -> 12%
where the time goes in v1:
time: 546 us; the launch traced here: 536 us
  waiting for transfers between devices  192 us (35%)
  starting transfers between devices  135 us (25%)
  Pallas kernels  82.4 us (15%)
  matrix products  62.1 us (11%)
  local copies, waits for them, and re-layouts  31.1 us (6%)
  other arithmetic  31.1 us (6%)
    dot_general x15, matrix products, dot(): lax.dot_general(a, b, ((dims[:1], dims[1:]), ((), ())), preferred_element...  62.1 us
    ppermute x24, waiting for transfers between devices, left(): return lax.ppermute(v, 'x', [(i, (i - 1) % size) for i in range(size)])  56.3 us
    ppermute x24, starting transfers between devices, left(): return lax.ppermute(v, 'x', [(i, (i - 1) % size) for i in range(size)])  50.1 us
    ppermute x11, waiting for transfers between devices, flip(): return lax.ppermute(v, 'zl', [(0, 1), (1, 0)])  46.4 us
    ppermute x23, waiting for transfers between devices, right(): return lax.ppermute(v, 'x', [(i, (i + 1) % size) for i in range(size)])  33 us
    ppermute x10, starting transfers between devices, down(): return lax.ppermute(v, 'y', [(i, (i - 1) % size) for i in range(size)])  25.5 us
    ppermute x10, waiting for transfers between devices, up(): return lax.ppermute(v, 'y', [(i, (i + 1) % size) for i in range(size)])  24.9 us
    ppermute x4, waiting for transfers between devices, hop(): return lax.ppermute(v, 'zh', [(0, 1), (1, 0)])  21.2 us
  transfers between devices with their start and end apart: 99, of which 47 were waited for; matrix products, arithmetic and copies ran while one was open for 14% of the time, Pallas kernels for 12%

profile of v1, /device:TPU:0, one launch (start us, length us, event | category | flops | bytes accessed | tf_op | source)
XLA Modules:
  0.0 536.1 jit_solution(16271183106547923116)
XLA Ops:
  8.2 5.7 %all-to-all-start = ((bf16[8,48,1152]{2,1,0:T(8,128)(2,1)}), bf16[8,48,1152]{2,1,0:T(8,128)(2,1)}, u32[]{:S(2)}, u32[]{:S(2)}) async-start(bf16[8,48,1152]{2,1,0:T(8,128)(2,1)} %shard_map.241), calls=%async_computation | async-start | bytes 1769472 | tf_op jit(solution)/shard_map/all_to_all | solution.py:675
  19.2 17.8 %collective-permute-done.refs_4_ = bf16[128,2048]{1,0:T(8,128)(2,1)S(1)} collective-permute-done((bf16[128,2048]{1,0:T(8,128)(2,1)S(1)}, bf16[128,2048]{1,0:T(8,128)(2,1)S(1)}, u32[]{:S(2)}, u32[]{:S(2)}) %collective-permute-start) | collective-permute-done | bytes 524320 | tf_op jit(solution)/shard_map/ppermute | solution.py:62
  46.7 6.2 %collective-permute-done.3.refs_2_ = bf16[128,2048]{1,0:T(8,128)(2,1)S(1)} collective-permute-done((bf16[128,2048]{1,0:T(8,128)(2,1)}, bf16[128,2048]{1,0:T(8,128)(2,1)S(1)}, u32[]{:S(2)}, u32[]{:S(2)}) %collective-permute-start.3) | collective-permute-done | bytes 524320 | tf_op jit(solution)/shard_map/ppermute | solution.py:53
  82.0 5.8 %shard_map.242.normed_ref = bf16[1024,2048]{1,0:T(8,128)(2,1)} custom-call(f32[1,2048]{1,0:T(1,128)} %bitcast.159, bf16[128,2048]{1,0:T(8,128)(2,1)} %refs_0_.1, bf16[128,2048]{1,0:T(8,128)(2,1)} %collective-permute-done.2.refs_1_, bf16[128,2048]{1,0:T(8,128)(2,1)} %copy-done.47, bf16[128,2048]{1,0:T(8,128)(2,1)} %copy-done.46, ...), custom_call_target="tpu_custom_call" | custom-call | bytes 8388608 | tf_op jit(solution)/shard_map/pallas_call | solution.py:702
  98.7 8.2 %fusion.34.pre_ref = f32[1024,1024]{1,0:T(8,128)} fusion(bf16[1024,2048]{1,0:T(8,128)(2,1)S(1)} %copy-done.10, bf16[2048,1024]{1,0:T(8,128)(2,1)} %get-tuple-element.199.cat_ref), kind=kOutput, calls=%fused_computation.160 | convolution fusion | flops 4294967296 | bytes 12582912 | tf_op jit(solution)/shard_map/dot_general | solution.py:48
  106.9 9.1 %shard_map.244 = (bf16[1024,384]{1,0:T(8,128)(2,1)}, bf16[1024,512]{1,0:T(8,128)(2,1)}, bf16[1024,512]{1,0:T(8,128)(2,1)}, bf16[1024,128]{1,0:T(8,128)(2,1)}, f3...) custom-call(s32[5]{0:T(128)} %stack.23.at_ref, f32[1024,1024]{1,0:T(8,128)} %fusion.34.pre_ref, ...), custom_call_target="tpu_custom_call" | custom-call | bytes 10485760 | tf_op jit(solution)/shard_map/pallas_call | solution.py:711
  124.4 9.2 %collective-permute-done.23 = bf16[128,2048]{1,0:T(8,128)(2,1)S(1)} collective-permute-done((bf16[128,2048]{1,0:T(8,128)(2,1)S(1)}, bf16[128,2048]{1,0:T(8,128)(2,1)S(1)}, u32[]{:S(2)}, u32[]{:S(2)}) %collective-permute-start.23) | collective-permute-done | bytes 524320 | tf_op jit(solution)/shard_map/ppermute | solution.py:58
  139.1 6.0 %collective-permute-done.26 = bf16[128,2048]{1,0:T(8,128)(2,1)S(1)} collective-permute-done((bf16[128,2048]{1,0:T(8,128)(2,1)S(1)}, bf16[128,2048]{1,0:T(8,128)(2,1)S(1)}, u32[]{:S(2)}, u32[]{:S(2)}) %collective-permute-start.26) | collective-permute-done | bytes 524320 | tf_op jit(solution)/shard_map/ppermute | solution.py:53
  181.5 6.9 %collective-permute-done.35.refs_5_ = bf16[128,2048]{1,0:T(8,128)(2,1)} collective-permute-done((bf16[128,2048]{1,0:T(8,128)(2,1)}, bf16[128,2048]{1,0:T(8,128)(2,1)}, u32[]{:S(2)}, u32[]{:S(2)}) %collective-permute-start.35) | collective-permute-done | bytes 524320 | tf_op jit(solution)/shard_map/ppermute | solution.py:58
  205.4 5.2 fusion.35
  213.9 6.0 %multiply_convert_fusion = (bf16[1024,704]{0,1:T(8,128)(2,1)}, bf16[1024,704]{0,1:T(8,128)(2,1)S(1)}, bf16[1024,704]{0,1:T(8,128)(2,1)S(1)}) fusion(f32[1024,704]{0,1:T(8,128)S(1)} %fusion.35, f32[1024,704]{0,1:T(8,128)S(1)} %fusion.36, f32[1024]{0:T(1024)S(1)} %bitcast.169, f32[1024]{0:T(1024)S(1)} %bitcast.168, pred[704]{0:T(1024)(128)(4,1)S(1)} %get-tuple-element.449, ...), kind=kOutput, calls=%fused_computation.9 | convolution fusion | flops 2967207936 | bytes 17180032 | tf_op jit(solution)/shard_map/dot_general | solution.py:48
  219.8 5.8 %fusion.37 = f32[1024,2048]{1,0:T(8,128)} fusion(bf16[1024,704]{0,1:T(8,128)(2,1)S(1)} %get-tuple-element.231, bf16[704,2048]{1,0:T(8,128)(2,1)S(1)} %bitcast.173), kind=kOutput, calls=%fused_computation.163 | convolution fusion | flops 2952790016 | bytes 12713984 | tf_op jit(solution)/shard_map/dot_general | solution.py:48
  225.6 6.0 %add_convert_fusion.1 = bf16[1024,2048]{1,0:T(8,128)(2,1)S(1)} fusion(f32[1024,2048]{1,0:T(8,128)} %fusion.37, bf16[1024,704]{0,1:T(8,128)(2,1)S(1)} %get-tuple-element.232, bf16[704,2048]{1,0:T(8,128)(2,1)S(1)} %bitcast.175), kind=kOutput, calls=%fused_computation.1 | convolution fusion | flops 2956984320 | bytes 16908288 | tf_op jit(solution)/shard_map/dot_general | solution.py:48
  253.7 8.0 %collective-permute-done.40 = bf16[128,2048]{1,0:T(8,128)(2,1)S(1)} collective-permute-done((bf16[128,2048]{1,0:T(8,128)(2,1)S(1)}, bf16[128,2048]{1,0:T(8,128)(2,1)S(1)}, u32[]{:S(2)}, u32[]{:S(2)}) %collective-permute-start.40) | collective-permute-done | bytes 524320 | tf_op jit(solution)/shard_map/ppermute | solution.py:62
  280.9 6.6 %collective-permute-done.46.refs_4_ = bf16[128,2048]{1,0:T(8,128)(2,1)S(1)} collective-permute-done((bf16[128,2048]{1,0:T(8,128)(2,1)S(1)}, bf16[128,2048]{1,0:T(8,128)(2,1)S(1)}, u32[]{:S(2)}, u32[]{:S(2)}) %collective-permute-start.46) | collective-permute-done | bytes 524320 | tf_op jit(solution)/shard_map/ppermute | solution.py:62
  294.3 8.5 %collective-permute-done.51.refs_5_ = bf16[128,2048]{1,0:T(8,128)(2,1)S(1)} collective-permute-done((bf16[128,2048]{1,0:T(8,128)(2,1)S(1)}, bf16[128,2048]{1,0:T(8,128)(2,1)S(1)}, u32[]{:S(2)}, u32[]{:S(2)}) %collective-permute-start.51) | collective-permute-done | bytes 524320 | tf_op jit(solution)/shard_map/ppermute | solution.py:58
  308.1 8.0 %collective-permute-done.52.refs_6_ = bf16[128,2048]{1,0:T(8,128)(2,1)S(1)} collective-permute-done((bf16[128,2048]{1,0:T(8,128)(2,1)S(1)}, bf16[128,2048]{1,0:T(8,128)(2,1)S(1)}, u32[]{:S(2)}, u32[]{:S(2)}) %collective-permute-start.52) | collective-permute-done | bytes 524320 | tf_op jit(solution)/shard_map/ppermute | solution.py:58
  344.1 12.9 %shard_map.249 = (bf16[1024,1024]{1,0:T(8,128)(2,1)}, bf16[1024,512]{1,0:T(8,128)(2,1)}) custom-call(s32[5]{0:T(128)} %stack.23.at_ref, bf16[1024,256]{1,0:T(8,128)(2,1)} %convolution_convert_fusion.7.gctx_ref, bf16[1024,384]{1,0:T(8,128)(2,1)} %get-tuple-element.263.q_ref, bf16[1024,512]{1,0:T(8,128)(2,1)} %get-tuple-element.264.kv_ref, ...), custom_call_target="tpu_custom_call" | custom-call | bytes 15728640 | tf_op jit(solution)/shard_map/pallas_call | solution.py:788
  366.7 10.9 %shard_map.250 = (bf16[4,10,32,1152]{3,2,1,0:T(8,128)(2,1)S(1)}, bf16[4,10,32,1152]{3,2,1,0:T(8,128)(2,1)S(1)}) custom-call(s32[5]{0:T(128)S(1)} %copy-done.5, bf16[1024,2048]{1,0:T(8,128)(2,1)} %shard_map.242.normed_ref, bf16[1024,1024]{1,0:T(8,128)(2,1)S(1)} %copy-done.3, bf16[2048,1024]{1,0:T(8,128)(2,1)} %get-tuple-element.199.cat_ref, ...), custom_call_target="tpu_custom_call" | custom-call | bytes 16777216 | tf_op jit(solution)/shard_map/pallas_call | solution.py:811
  377.6 5.4 %collective-permute-done.61 = bf16[1056,512]{1,0:T(8,128)(2,1)} collective-permute-done((bf16[1056,512]{1,0:T(8,128)(2,1)}, bf16[1056,512]{1,0:T(8,128)(2,1)}, u32[]{:S(2)}, u32[]{:S(2)}) %collective-permute-start.61) | collective-permute-done | bytes 1081376 | tf_op jit(solution)/shard_map/ppermute | solution.py:173
  401.2 8.3 %collective-permute-done.63 = bf16[528,512]{1,0:T(8,128)(2,1)S(1)} collective-permute-done((bf16[528,512]{1,0:T(8,128)(2,1)S(1)}, bf16[528,512]{1,0:T(8,128)(2,1)S(1)}, u32[]{:S(2)}, u32[]{:S(2)}) %collective-permute-start.63) | collective-permute-done | bytes 540704 | tf_op jit(solution)/shard_map/ppermute | solution.py:168
  433.6 9.5 %collective-permute-done.69 = bf16[10,32,1152]{2,1,0:T(8,128)(2,1)S(1)} collective-permute-done((bf16[10,32,1152]{2,1,0:T(8,128)(2,1)S(1)}, bf16[10,32,1152]{2,1,0:T(8,128)(2,1)S(1)}, u32[]{:S(2)}, u32[]{:S(2)}) %collective-permute-start.69) | collective-permute-done | bytes 737312 | tf_op jit(solution)/shard_map/ppermute | solution.py:173
  458.8 6.3 %collective-permute-done.71 = bf16[10,16,1152]{2,1,0:T(8,128)(2,1)S(1)} collective-permute-done((bf16[10,16,1152]{2,1,0:T(8,128)(2,1)S(1)}, bf16[10,16,1152]{2,1,0:T(8,128)(2,1)S(1)}, u32[]{:S(2)}, u32[]{:S(2)}) %collective-permute-start.71) | collective-permute-done | bytes 368672 | tf_op jit(solution)/shard_map/ppermute | solution.py:168
  492.5 6.6 %collective-permute-done.82 = bf16[16,6784]{1,0:T(8,128)(2,1)S(1)} collective-permute-done((bf16[16,6784]{1,0:T(8,128)(2,1)S(1)}, bf16[16,6784]{1,0:T(8,128)(2,1)S(1)}, u32[]{:S(2)}, u32[]{:S(2)}) %collective-permute-start.82) | collective-permute-done | bytes 217120 | tf_op jit(solution)/shard_map/ppermute | solution.py:168
  (489 shorter events, 344.4 us)
Async XLA Ops:
  8.2 30.8 %all-to-all-start = ((bf16[8,48,1152]{2,1,0:T(8,128)(2,1)}), bf16[8,48,1152]{2,1,0:T(8,128)(2,1)}, u32[]{:S(2)}, u32[]{:S(2)}) async-start(bf16[8,48,1152]{2,1,0:T(8,128)(2,1)} %shard_map.241), calls=%async_computation | async-start | bytes 1769472 | tf_op jit(solution)/shard_map/all_to_all | solution.py:675
  13.9 23.1 %collective-permute-start = (bf16[128,2048]{1,0:T(8,128)(2,1)S(1)}, bf16[128,2048]{1,0:T(8,128)(2,1)S(1)}, u32[]{:S(2)}, u32[]{:S(2)}) collective-permute-start(bf16[128,2048]{1,0:T(8,128)(2,1)S(1)} %copy-done.13), channel_id=1, source_target_pairs={{0,1},{1,0},{2,3},{3,2},{4,5},{5,4},{6,7},{7,6},{8,9},{9,8},{10,11... | collective-permute-start | bytes 1572872 | tf_op jit(solution)/shard_map/ppermute | solution.py:62
  15.9 22.3 %collective-permute-start.1 = (bf16[128,2048]{1,0:T(8,128)(2,1)S(1)}, bf16[128,2048]{1,0:T(8,128)(2,1)S(1)}, u32[]{:S(2)}, u32[]{:S(2)}) collective-permute-start(bf16[128,2048]{1,0:T(8,128)(2,1)S(1)} %copy-done.13), channel_id=1, source_target_pairs={{0,2},{2,4},{4,6},{6,0},{1,3},{3,5},{5,7},{7,1},{8,10},{10,12},{12... | collective-permute-start | bytes 1572872 | tf_op jit(solution)/shard_map/ppermute | solution.py:53
  46.7 24.2 %collective-permute-start.7 = (bf16[8,32,1152]{2,1,0:T(8,128)(2,1)S(1)}, bf16[8,32,1152]{2,1,0:T(8,128)(2,1)}, u32[]{:S(2)}, u32[]{:S(2)}) collective-permute-start(bf16[8,32,1152]{2,1,0:T(8,128)(2,1)S(1)} %slice.432.refs_0_), channel_id=1, source_target_pairs={{0,8},{8,0},{1,9},{9,1},{2,10},{10,2},{3,11},{11,3},{4,12},{12,4},... | collective-permute-start | bytes 1769480 | tf_op jit(solution)/shard_map/ppermute | solution.py:164
  87.9 28.1 %collective-permute-start.17 = (bf16[128,2048]{1,0:T(8,128)(2,1)S(1)}, bf16[128,2048]{1,0:T(8,128)(2,1)S(1)}, u32[]{:S(2)}, u32[]{:S(2)}) collective-permute-start(bf16[128,2048]{1,0:T(8,128)(2,1)S(1)} %copy-done.16), channel_id=1, source_target_pairs={{0,6},{2,0},{4,2},{6,4},{1,7},{3,1},{5,3},{7,5},{8,14},{10,8},{12,... | collective-permute-start | bytes 1572872 | tf_op jit(solution)/shard_map/ppermute | solution.py:58
  89.7 26.3 %collective-permute-start.20 = (bf16[128,2048]{1,0:T(8,128)(2,1)}, bf16[128,2048]{1,0:T(8,128)(2,1)}, u32[]{:S(2)}, u32[]{:S(2)}) collective-permute-start(bf16[128,2048]{1,0:T(8,128)(2,1)} %collective-permute-done.19.refs_6_), channel_id=1, source_target_pairs={{0,2},{2,4},{4,6},{6,0},{1,3},{3,5},{5,7},{7,1},{8,10},{10,12},{12... | collective-permute-start | bytes 1572872 | tf_op jit(solution)/shard_map/ppermute | solution.py:53
  90.0 26.1 %collective-permute-start.22 = (bf16[128,2048]{1,0:T(8,128)(2,1)}, bf16[128,2048]{1,0:T(8,128)(2,1)}, u32[]{:S(2)}, u32[]{:S(2)}) collective-permute-start(bf16[128,2048]{1,0:T(8,128)(2,1)} %collective-permute-done.19.refs_6_), channel_id=1, source_target_pairs={{0,1},{1,0},{2,3},{3,2},{4,5},{5,4},{6,7},{7,6},{8,9},{9,8},{10,11... | collective-permute-start | bytes 1572872 | tf_op jit(solution)/shard_map/ppermute | solution.py:62
  121.2 23.9 %collective-permute-start.26 = (bf16[128,2048]{1,0:T(8,128)(2,1)S(1)}, bf16[128,2048]{1,0:T(8,128)(2,1)S(1)}, u32[]{:S(2)}, u32[]{:S(2)}) collective-permute-start(bf16[128,2048]{1,0:T(8,128)(2,1)S(1)} %get-tuple-element.419), channel_id=1, source_target_pairs={{0,2},{2,4},{4,6},{6,0},{1,3},{3,5},{5,7},{7,1},{8,10},{10,12},{12... | collective-permute-start | bytes 1572872 | tf_op jit(solution)/shard_map/ppermute | solution.py:53
  121.3 23.8 %collective-permute-start.27 = (bf16[128,2048]{1,0:T(8,128)(2,1)S(1)}, bf16[128,2048]{1,0:T(8,128)(2,1)S(1)}, u32[]{:S(2)}, u32[]{:S(2)}) collective-permute-start(bf16[128,2048]{1,0:T(8,128)(2,1)S(1)} %get-tuple-element.418), channel_id=1, source_target_pairs={{0,6},{2,0},{4,2},{6,4},{1,7},{3,1},{5,3},{7,5},{8,14},{10,8},{12,... | collective-permute-start | bytes 1572872 | tf_op jit(solution)/shard_map/ppermute | solution.py:58
  271.6 35.0 %collective-permute-start.50 = (bf16[4,1056,512]{2,1,0:T(8,128)(2,1)}, bf16[4,1056,512]{2,1,0:T(8,128)(2,1)S(1)}, u32[]{:S(2)}, u32[]{:S(2)}) collective-permute-start(bf16[4,1056,512]{2,1,0:T(8,128)(2,1)} %get-tuple-element.248), channel_id=1, source_target_pairs={{0,8},{8,0},{1,9},{9,1},{2,10},{10,2},{3,11},{11,3},{4,12},{12,4},... | collective-permute-start | bytes 12976136 | tf_op jit(solution)/shard_map/ppermute | solution.py:164
  294.3 21.9 %collective-permute-start.53 = (bf16[128,2048]{1,0:T(8,128)(2,1)S(1)}, bf16[128,2048]{1,0:T(8,128)(2,1)S(1)}, u32[]{:S(2)}, u32[]{:S(2)}) collective-permute-start(bf16[128,2048]{1,0:T(8,128)(2,1)S(1)} %collective-permute-done.46.refs_4_), channel_id=1, source_target_pairs={{0,2},{2,4},{4,6},{6,0},{1,3},{3,5},{5,7},{7,1},{8,10},{10,12},{12... | collective-permute-start | bytes 1572872 | tf_op jit(solution)/shard_map/ppermute | solution.py:53
  326.9 30.1 %collective-permute-start.54 = (bf16[528,512]{1,0:T(8,128)(2,1)}, bf16[528,512]{1,0:T(8,128)(2,1)}, u32[]{:S(2)}, u32[]{:S(2)}) collective-permute-start(bf16[528,512]{1,0:T(8,128)(2,1)} %get-tuple-element.389), channel_id=1, source_target_pairs={{0,48},{16,0},{32,16},{48,32},{1,49},{17,1},{33,17},{49,33},{2,50}... | collective-permute-start | bytes 1622024 | tf_op jit(solution)/shard_map/ppermute | solution.py:178
  329.7 27.4 %collective-permute-start.55 = (bf16[528,512]{1,0:T(8,128)(2,1)}, bf16[528,512]{1,0:T(8,128)(2,1)}, u32[]{:S(2)}, u32[]{:S(2)}) collective-permute-start(bf16[528,512]{1,0:T(8,128)(2,1)} %get-tuple-element.388), channel_id=1, source_target_pairs={{0,16},{16,32},{32,48},{48,0},{1,17},{17,33},{33,49},{49,1},{2,18}... | collective-permute-start | bytes 1622024 | tf_op jit(solution)/shard_map/ppermute | solution.py:173
  329.7 27.3 %collective-permute-start.57 = (bf16[128,2048]{1,0:T(8,128)(2,1)}, bf16[128,2048]{1,0:T(8,128)(2,1)}, u32[]{:S(2)}, u32[]{:S(2)}) collective-permute-start(bf16[128,2048]{1,0:T(8,128)(2,1)} %get-tuple-element.270), channel_id=1, source_target_pairs={{0,2},{2,4},{4,6},{6,0},{1,3},{3,5},{5,7},{7,1},{8,10},{10,12},{12... | collective-permute-start | bytes 1572872 | tf_op jit(solution)/shard_map/ppermute | solution.py:53
  329.7 27.3 %collective-permute-start.58 = (bf16[128,2048]{1,0:T(8,128)(2,1)}, bf16[128,2048]{1,0:T(8,128)(2,1)}, u32[]{:S(2)}, u32[]{:S(2)}) collective-permute-start(bf16[128,2048]{1,0:T(8,128)(2,1)} %get-tuple-element.271), channel_id=1, source_target_pairs={{0,2},{2,4},{4,6},{6,0},{1,3},{3,5},{5,7},{7,1},{8,10},{10,12},{12... | collective-permute-start | bytes 1572872 | tf_op jit(solution)/shard_map/ppermute | solution.py:53
  334.5 22.6 %collective-permute-start.59 = (bf16[128,2048]{1,0:T(8,128)(2,1)}, bf16[128,2048]{1,0:T(8,128)(2,1)}, u32[]{:S(2)}, u32[]{:S(2)}) collective-permute-start(bf16[128,2048]{1,0:T(8,128)(2,1)} %get-tuple-element.272), channel_id=1, source_target_pairs={{0,6},{2,0},{4,2},{6,4},{1,7},{3,1},{5,3},{7,5},{8,14},{10,8},{12,... | collective-permute-start | bytes 1572872 | tf_op jit(solution)/shard_map/ppermute | solution.py:58
  359.7 23.4 %collective-permute-start.61 = (bf16[1056,512]{1,0:T(8,128)(2,1)}, bf16[1056,512]{1,0:T(8,128)(2,1)}, u32[]{:S(2)}, u32[]{:S(2)}) collective-permute-start(bf16[1056,512]{1,0:T(8,128)(2,1)} %pad_maximum_fusion.1), channel_id=1, source_target_pairs={{0,16},{16,32},{32,48},{48,0},{1,17},{17,33},{33,49},{49,1},{2,18}... | collective-permute-start | bytes 3244040 | tf_op jit(solution)/shard_map/ppermute | solution.py:173
  362.4 22.1 %collective-permute-start.60 = (bf16[1056,512]{1,0:T(8,128)(2,1)}, bf16[1056,512]{1,0:T(8,128)(2,1)}, u32[]{:S(2)}, u32[]{:S(2)}) collective-permute-start(bf16[1056,512]{1,0:T(8,128)(2,1)} %pad_maximum_fusion), channel_id=1, source_target_pairs={{0,48},{16,0},{32,16},{48,32},{1,49},{17,1},{33,17},{49,33},{2,50}... | collective-permute-start | bytes 3244040 | tf_op jit(solution)/shard_map/ppermute | solution.py:178
  384.5 25.0 %collective-permute-start.62 = (bf16[4,10,32,1152]{3,2,1,0:T(8,128)(2,1)S(1)}, bf16[4,10,32,1152]{3,2,1,0:T(8,128)(2,1)S(1)}, u32[]{:S(2)}, u32[]{:S(2)}) collective-permute-start(bf16[4,10,32,1152]{3,2,1,0:T(8,128)(2,1)S(1)} %get-tuple-element.285), channel_id=1, source_target_pairs={{0,8},{8,0},{1,9},{9,1},{2,10},{10,2},{3,11},{11,3},{4,12},{12,4},... | collective-permute-start | bytes 8847368 | tf_op jit(solution)/shard_map/ppermute | solution.py:164
  390.6 54.1 %collective-permute-start.72 = (bf16[128,2048]{1,0:T(8,128)(2,1)S(1)}, bf16[128,2048]{1,0:T(8,128)(2,1)S(1)}, u32[]{:S(2)}, u32[]{:S(2)}) collective-permute-start(bf16[128,2048]{1,0:T(8,128)(2,1)S(1)} %get-tuple-element.399), channel_id=1, source_target_pairs={{0,6},{2,0},{4,2},{6,4},{1,7},{3,1},{5,3},{7,5},{8,14},{10,8},{12,... | collective-permute-start | bytes 1572872 | tf_op jit(solution)/shard_map/ppermute | solution.py:58
  416.2 32.4 %collective-permute-start.73 = (bf16[128,2048]{1,0:T(8,128)(2,1)S(1)}, bf16[128,2048]{1,0:T(8,128)(2,1)S(1)}, u32[]{:S(2)}, u32[]{:S(2)}) collective-permute-start(bf16[128,2048]{1,0:T(8,128)(2,1)S(1)} %get-tuple-element.398), channel_id=1, source_target_pairs={{0,2},{2,4},{4,6},{6,0},{1,3},{3,5},{5,7},{7,1},{8,10},{10,12},{12... | collective-permute-start | bytes 1572872 | tf_op jit(solution)/shard_map/ppermute | solution.py:53
  448.6 33.0 %collective-permute-start.77 = (bf16[1056,512]{1,0:T(8,128)(2,1)S(1)}, bf16[1056,512]{1,0:T(8,128)(2,1)S(1)}, u32[]{:S(2)}, u32[]{:S(2)}) collective-permute-start(bf16[1056,512]{1,0:T(8,128)(2,1)S(1)} %pad_maximum_fusion.2.refs_0_), channel_id=1, source_target_pairs={{0,48},{16,0},{32,16},{48,32},{1,49},{17,1},{33,17},{49,33},{2,50}... | collective-permute-start | bytes 3244040 | tf_op jit(solution)/shard_map/ppermute | solution.py:178
  450.7 30.9 %collective-permute-start.78 = (bf16[1056,512]{1,0:T(8,128)(2,1)S(1)}, bf16[1056,512]{1,0:T(8,128)(2,1)S(1)}, u32[]{:S(2)}, u32[]{:S(2)}) collective-permute-start(bf16[1056,512]{1,0:T(8,128)(2,1)S(1)} %pad_maximum_fusion.2.refs_0_), channel_id=1, source_target_pairs={{0,16},{16,32},{32,48},{48,0},{1,17},{17,33},{33,49},{49,1},{2,18}... | collective-permute-start | bytes 3244040 | tf_op jit(solution)/shard_map/ppermute | solution.py:173
  454.9 26.7 %collective-permute-start.79 = (bf16[1056,512]{1,0:T(8,128)(2,1)S(1)}, bf16[1056,512]{1,0:T(8,128)(2,1)}, u32[]{:S(2)}, u32[]{:S(2)}) collective-permute-start(bf16[1056,512]{1,0:T(8,128)(2,1)S(1)} %pad_maximum_fusion.2.refs_0_), channel_id=1, source_target_pairs={{0,8},{8,0},{1,9},{9,1},{2,10},{10,2},{3,11},{11,3},{4,12},{12,4},... | collective-permute-start | bytes 3244040 | tf_op jit(solution)/shard_map/ppermute | solution.py:164
  (156 other events, 1867.7 us)
